TPU v7x, 256 devices: a whole 4x4x8 slice. The times are simulated.
256 devices in a mesh: gx: 16 (over z_hi, y), gy: 16 (over z_lo, x, core).
Axes of the slice: x: 4, y: 4, z: 8 (z_hi: 4, z_lo: 2; z = z_hi * 2 + z_lo), core: 2. Of those that a mesh axis runs over, the one named last changes fastest.
Arguments:
- face_trans: float32 [3, 256, 256, 128], P(None, 'gx', 'gy'), may hold values from 0.002 to 0.2
- partition: int32 [256, 256, 128], P('gx', 'gy'), may hold values from 0 to 26, as said below
- support_pad: int32 [6, 32, 32, 16], P(None, 'gx', 'gy'), may hold values from 1 to 3
- owners: int32 [16, 16, 64, 1], P('gx', 'gy'), may hold values from 0 to 15; in each aligned block of 64 rows (0 to 63, 64 to 127, ..., all dimensions but the last counted through in order) at most 8 rows name the same one
Outputs:
- prolongation: float32 [8, 256, 256, 128], P(None, 'gx', 'gy')
- coarse_rows: float32 [16, 16, 27, 128], P('gx', 'gy')
Inputs may be any that keep to these rules, and one draw needn't show every extreme that they name: `partition`: each cell's own block is the block holding a position that lies in the grid and differs from the cell by at most one cell in each dimension. `owners`: among the blocks of one device, no owner index is named more than 8 times, a bound that some block reaches.
All inputs are finite; a program needn't handle non-finite values.
Results may differ from a plain program's by a relative error of at most 0.0001.
Values sent between devices are 32-bit elements; how exact they have to be, the bound alone decides.
A program may use at most 128 MiB of HBM per device.

v0:
```python
import jax
import jax.numpy as jnp
from jax import lax
from jax.sharding import PartitionSpec as P

B = 8
H = 4
ITERS = 2
CX = 16
CY = 16
CZ = 128
NBXD = 2
NBYD = 2
NBZ = 16
NB_DEV = 64


relax = 2.0 / 3.0
highest = lax.Precision.HIGHEST


def padded_2(block, sides, width):
    for axis, dim in sides:
        count = lax.axis_size(axis)
        forward = [(i, i + 1) for i in range(count - 1)]
        backward = [(target, source) for source, target in forward]
        low = lax.ppermute(
            lax.slice_in_dim(block, block.shape[dim] - width, None, axis=dim), axis, forward
        )
        high = lax.ppermute(lax.slice_in_dim(block, 0, width, axis=dim), axis, backward)
        block = jnp.concatenate([low, block, high], axis=dim)
    return block


def passed_along(block, axis, distance):
    devices = range(lax.axis_size(axis))
    route = [(i - distance, i) for i in devices if i - distance in devices]
    return lax.ppermute(block, axis, route)


def slot_cover(position, parity):
    blocks = position // B
    toward = jnp.where(position % B >= H, 1, -1)
    cover_block = jnp.where(blocks % 2 == parity, blocks, blocks + toward)
    offset = (position + H + parity * B) % (2 * B)
    return (cover_block, offset)


def stencil(padded, faces, diagonal):
    west_trans, east_trans, south_trans, north_trans, bottom_trans, top_trans = faces
    centre = padded[..., 1:-1, 1:-1, :]
    zero_layer = jnp.zeros_like(centre[..., :1])
    above = jnp.concatenate([centre[..., 1:], zero_layer], -1)
    below = jnp.concatenate([zero_layer, centre[..., :-1]], -1)
    return (
        diagonal * centre
        - east_trans * padded[..., 2:, 1:-1, :]
        - west_trans * padded[..., :-2, 1:-1, :]
        - north_trans * padded[..., 1:-1, 2:, :]
        - south_trans * padded[..., 1:-1, :-2, :]
        - top_trans * above
        - bottom_trans * below
    )


def coarse_table(halves, margin, span):
    half_index = jnp.arange(halves, dtype=jnp.int32)
    blocks = half_index // 2
    toward = jnp.where(half_index % 2 == 1, 1, -1)
    bit_values = jnp.arange(2, dtype=jnp.int32)
    cover_block = jnp.where(
        blocks[None, :] % 2 == bit_values[:, None],
        blocks[None, :],
        blocks[None, :] + toward[None, :],
    )
    target = blocks[None, :] + bit_values[:, None] * toward[None, :]
    places = jnp.arange(span, dtype=jnp.int32)
    codes = jnp.arange(3, dtype=jnp.int32)
    hit_target = target[:, :, None] + margin == places[None, None, :]
    hit_code = (
        cover_block[:, None, :, None] - target[None, :, :, None] + 1 == codes[None, None, None, :]
    )
    return (hit_target[None, :, :, :, None] & hit_code[:, :, :, None, :]).astype(jnp.float32)


def fold_edges(values, axis):
    length = values.shape[axis]
    row_count = length - 4
    inner_rows = lax.slice_in_dim(values, 2, length - 2, axis=axis)
    leading_row = lax.slice_in_dim(values, 0, 1, axis=axis)
    trailing_row = lax.slice_in_dim(values, length - 1, length, axis=axis)
    front_pad = [(0, 0)] * values.ndim
    back_pad = [(0, 0)] * values.ndim
    front_pad[axis] = (0, row_count - 1)
    back_pad[axis] = (row_count - 1, 0)
    return inner_rows + jnp.pad(leading_row, front_pad) + jnp.pad(trailing_row, back_pad)


def on_device(face_trans, partition, support_pad, owners):
    size_y = lax.axis_size("gy")
    first_x = lax.axis_index("gx") * CX
    first_y = lax.axis_index("gy") * CY
    width_x = CX * lax.axis_size("gx")
    width_y = CY * size_y
    pad_cycle = padded_2(support_pad, (("gx", 1), ("gy", 2)), 1)
    pad_cycle = jnp.pad(pad_cycle, ((0, 0), (0, 0), (0, 0), (1, 1))).astype(jnp.float32)
    extent = 0
    west_layer = passed_along(face_trans[0, CX - 1 :], "gx", 1)
    south_layer = passed_along(face_trans[1, :, CY - 1 :], "gy", 1)

    def widen(values):
        return padded_2(values, (("gx", 1), ("gy", 2)), 1)

    local_x = jnp.arange(CX + 2 * extent, dtype=jnp.int32) - extent
    local_y = jnp.arange(CY + 2 * extent, dtype=jnp.int32) - extent
    along_z = jnp.arange(CZ, dtype=jnp.int32)
    global_x = local_x + first_x
    global_y = local_y + first_y
    inside = ((global_x >= 0) & (global_x < width_x))[:, None, None] & (
        (global_y >= 0) & (global_y < width_y)
    )[None, :, None]
    east_trans = face_trans[0] * (global_x < width_x - 1)[:, None, None]
    north_trans = face_trans[1] * (global_y < width_y - 1)[None, :, None]
    top_trans = face_trans[2] * (along_z < CZ - 1)[None, None, :]
    west_trans = jnp.concatenate([west_layer, east_trans[:-1]], 0)
    south_trans = jnp.concatenate([south_layer, north_trans[:, :-1]], 1)
    bottom_trans = jnp.pad(top_trans[:, :, :-1], ((0, 0), (0, 0), (1, 0)))
    faces = (west_trans, east_trans, south_trans, north_trans, bottom_trans, top_trans)
    diagonal = west_trans + east_trans + south_trans + north_trans + bottom_trans + top_trans
    safe_diagonal = jnp.where(inside, diagonal, 1.0)
    part_x = (local_x // B)[:, None, None] + partition // 9 - 1
    part_y = (local_y // B)[None, :, None] + partition // 3 % 3 - 1
    part_z = (along_z // B)[None, None, :] + partition % 3 - 1
    support_list = []
    start_list = []
    for slot_id in range(8):
        cover_x, offset_x = slot_cover(local_x, slot_id >> 2 & 1)
        cover_y, offset_y = slot_cover(local_y, slot_id >> 1 & 1)
        cover_z, offset_z = slot_cover(along_z, slot_id & 1)
        pick_x = (cover_x[:, None] + 1 == jnp.arange(NBXD + 2, dtype=jnp.int32)[None, :]).astype(
            jnp.float32
        )
        pick_y = (cover_y[:, None] + 1 == jnp.arange(NBYD + 2, dtype=jnp.int32)[None, :]).astype(
            jnp.float32
        )
        pick_z = (cover_z[:, None] + 1 == jnp.arange(NBZ + 2, dtype=jnp.int32)[None, :]).astype(
            jnp.float32
        )
        spread = jnp.einsum("cabd,xa->cxbd", pad_cycle, pick_x, precision=highest)
        spread = jnp.einsum("cxbd,yb->cxyd", spread, pick_y, precision=highest)
        spread = jnp.einsum("cxyd,zd->cxyz", spread, pick_z, precision=highest)
        near_x = offset_x[:, None, None]
        near_y = offset_y[None, :, None]
        near_z = offset_z[None, None, :]
        allowed = (
            (near_x + spread[0] >= H)
            & (near_x <= H + B - 1 + spread[1])
            & (near_y + spread[2] >= H)
            & (near_y <= H + B - 1 + spread[3])
            & (near_z + spread[4] >= H)
            & (near_z <= H + B - 1 + spread[5])
            & inside
        )
        support = allowed.astype(jnp.float32)
        start = (
            (cover_x[:, None, None] == part_x)
            & (cover_y[None, :, None] == part_y)
            & (cover_z[None, None, :] == part_z)
        ).astype(jnp.float32)
        support_list.append(support)
        start_list.append(start * support)
    support_all = jnp.stack(support_list)
    basis_slots = jnp.stack(start_list)
    for step_id in range(ITERS):
        applied = stencil(widen(basis_slots), faces, diagonal)
        updated = support_all * (basis_slots - relax * applied / safe_diagonal)
        slot_total = jnp.sum(updated, 0)
        basis_slots = updated / jnp.where(inside, slot_total, 1.0)
    applied = stencil(widen(basis_slots), faces, diagonal)
    move_code = (
        (partition // 9 != 1).astype(jnp.int32) * 4
        + (partition // 3 % 3 != 1).astype(jnp.int32) * 2
        + (partition % 3 != 1).astype(jnp.int32)
    )
    cube_list = []
    for move_id in range(8):
        picked = applied * (move_code == move_id)
        cube_list.append(picked.reshape(8, CX // H, H, CY // H, H, CZ // H, H).sum(axis=(2, 4, 6)))
    cube_sums = jnp.stack(cube_list, 1).reshape(2, 2, 2, 2, 2, 2, CX // H, CY // H, CZ // H)
    table_x = coarse_table(CX // H, 1, NBXD + 2)
    table_y = coarse_table(CY // H, 1, NBYD + 2)
    table_z = coarse_table(CZ // H, 0, NBZ)
    acc = jnp.einsum("abcdefxyz,adxio->bcefyzio", cube_sums, table_x, precision=highest)
    acc = jnp.einsum("bcefyzio,beyjp->cfzijop", acc, table_y, precision=highest)
    acc = jnp.einsum("cfzijop,cfzkr->oprijk", acc, table_z, precision=highest)
    acc = acc.reshape(27, NBXD + 2, NBYD + 2, NBZ)
    widened = padded_2(acc, (("gx", 1), ("gy", 2)), 1)
    folded = fold_edges(fold_edges(widened, 1), 2)
    rows_dev = folded.reshape(27, NB_DEV)
    capacity = max(2, 2 * NB_DEV // size_y)
    owner_ids = owners.reshape(NB_DEV)
    every_rows, every_owner = (
        lax.all_gather(rows_dev, "gy", axis=1, tiled=True),
        lax.all_gather(owner_ids.astype(jnp.float32)[None, :], "gy", axis=1, tiled=True),
    )
    own_index = lax.axis_index("gy").astype(jnp.float32)
    mine = (every_owner[0].reshape(size_y, NB_DEV) == own_index).astype(jnp.int32)
    ranks = jnp.cumsum(mine, 1) - mine
    placing = (
        mine[:, :, None]
        * (ranks[:, :, None] == jnp.arange(capacity, dtype=jnp.int32)[None, None, :])
    ).astype(jnp.float32)
    result = jnp.einsum(
        "ksl,slr->ksr", every_rows.reshape(27, size_y, NB_DEV), placing, precision=highest
    )
    result = result.reshape(27, size_y * capacity)
    return (basis_slots, result.reshape(1, 1, 27, size_y * capacity))


def solution(mesh):
    placed = (
        P(None, "gx", "gy", None),
        P("gx", "gy", None),
        P(None, "gx", "gy", None),
        P("gx", "gy", None, None),
    )
    return jax.shard_map(
        on_device,
        mesh=mesh,
        in_specs=placed,
        out_specs=(P(None, "gx", "gy", None), P("gx", "gy", None, None)),
        check_vma=False,
    )
```

profile of v0, /device:TPU:95, one launch (start us, length us, event | category | flops | bytes accessed | tf_op | source)
XLA Modules:
  0.0 340.7 jit_solution(9177167950392414581)
XLA Ops:
  9.8 7.6 %collective-permute-start.4 = (f32[1,16,128]{2,1,0:T(8,128)S(1)}, f32[1,16,128]{2,1,0:T(8,128)S(1)}, u32[]{:S(2)}, u32[]{:S(2)}) collective-permute-start(f32[1,16,128]{2,1,0:T(8,128)S(1)} %slice_bitcast_fusion.1), channel_id=1, source_target_pairs={{0,16},{16,32},{32,48},{48,64},{64,80},{80,96},{96,112},{112,128},... | collective-permute-start | bytes 24584 | tf_op jit(solution)/shard_map/ppermute | solution.py:38
  49.5 7.8 %collective-permute-start.7 = (f32[8,1,16,128]{3,2,1,0:T(8,128)S(1)}, f32[8,1,16,128]{3,2,1,0:T(8,128)S(1)}, u32[]{:S(2)}, u32[]{:S(2)}) collective-permute-start(f32[8,1,16,128]{3,2,1,0:T(8,128)S(1)} %get-tuple-element.48), channel_id=1, source_target_pairs={{0,16},{16,32},{32,48},{48,64},{64,80},{80,96},{96,112},{112,128},... | collective-permute-start | bytes 196616 | tf_op jit(solution)/shard_map/ppermute | solution.py:27
  70.9 7.8 %collective-permute-start.11 = (f32[8,1,16,128]{3,2,1,0:T(8,128)S(1)}, f32[8,1,16,128]{3,2,1,0:T(8,128)S(1)}, u32[]{:S(2)}, u32[]{:S(2)}) collective-permute-start(f32[8,1,16,128]{3,2,1,0:T(8,128)S(1)} %get-tuple-element.44), channel_id=1, source_target_pairs={{0,16},{16,32},{32,48},{48,64},{64,80},{80,96},{96,112},{112,128},... | collective-permute-start | bytes 196616 | tf_op jit(solution)/shard_map/ppermute | solution.py:27
  82.1 7.3 %collective-permute-start.13 = (f32[8,18,1,128]{3,2,1,0:T(1,128)S(1)}, f32[8,18,1,128]{3,2,1,0:T(1,128)S(1)}, u32[]{:S(2)}, u32[]{:S(2)}) collective-permute-start(f32[8,18,1,128]{3,2,1,0:T(1,128)S(1)} %get-tuple-element.30), channel_id=1, source_target_pairs={{0,1},{1,2},{2,3},{3,4},{4,5},{5,6},{6,7},{7,8},{8,9},{9,10},{10,1... | collective-permute-start | bytes 221192 | tf_op jit(solution)/shard_map/ppermute | solution.py:27
  94.1 8.2 %collective-permute-start.15 = (f32[8,1,16,128]{3,2,1,0:T(8,128)S(1)}, f32[8,1,16,128]{3,2,1,0:T(8,128)S(1)}, u32[]{:S(2)}, u32[]{:S(2)}) collective-permute-start(f32[8,1,16,128]{3,2,1,0:T(8,128)S(1)} %get-tuple-element.40), channel_id=1, source_target_pairs={{0,16},{16,32},{32,48},{48,64},{64,80},{80,96},{96,112},{112,128},... | collective-permute-start | bytes 196616 | tf_op jit(solution)/shard_map/ppermute | solution.py:27
  120.0 9.8 %copy.96 = f32[8,16,16,128]{0,3,2,1:T(8,128)} copy(f32[8,16,16,128]{3,2,1,0:T(8,128)} %get-tuple-element.39) | data formatting | bytes 2097152 | tf_op jit(solution)/shard_map/mul | solution.py:187
  129.9 9.5 %reduce_sum.92 = f32[8,4,4,32]{0,3,2,1:T(8,128)S(1)} reduce(f32[8,4,4,4,4,32,4]{0,6,5,4,3,2,1:T(4,128)} %bitcast.559, f32[]{:T(128)} %constant.554.clone.1), dimensions={2,4,6}, to_apply=%region_3.4 | reduce | flops 258048 | bytes 1064964 | tf_op jit(solution)/shard_map/reduce_sum | solution.py:188
  139.5 8.6 %copy.97 = f32[8,16,16,128]{0,3,2,1:T(8,128)} copy(f32[8,16,16,128]{3,2,1,0:T(8,128)S(1)} %copy-done.6) | data formatting | bytes 2097152 | tf_op jit(solution)/shard_map/mul | solution.py:187
  148.0 9.5 %reduce_sum.93 = f32[8,4,4,32]{0,3,2,1:T(8,128)S(1)} reduce(f32[8,4,4,4,4,32,4]{0,6,5,4,3,2,1:T(4,128)} %bitcast.560, f32[]{:T(128)} %constant.554.clone.1), dimensions={2,4,6}, to_apply=%region_4.5 | reduce | flops 258048 | bytes 1064964 | tf_op jit(solution)/shard_map/reduce_sum | solution.py:188
  157.6 8.6 %copy.98 = f32[8,16,16,128]{0,3,2,1:T(8,128)} copy(f32[8,16,16,128]{3,2,1,0:T(8,128)S(1)} %copy-done.5) | data formatting | bytes 2097152 | tf_op jit(solution)/shard_map/mul | solution.py:187
  166.2 9.5 %reduce_sum.94 = f32[8,4,4,32]{0,3,2,1:T(8,128)S(1)} reduce(f32[8,4,4,4,4,32,4]{0,6,5,4,3,2,1:T(4,128)} %bitcast.561, f32[]{:T(128)} %constant.554.clone.1), dimensions={2,4,6}, to_apply=%region_5.6 | reduce | flops 258048 | bytes 1064964 | tf_op jit(solution)/shard_map/reduce_sum | solution.py:188
  176.4 8.6 %copy.99 = f32[8,16,16,128]{0,3,2,1:T(8,128)} copy(f32[8,16,16,128]{3,2,1,0:T(8,128)S(1)} %copy-done.4) | data formatting | bytes 2097152 | tf_op jit(solution)/shard_map/mul | solution.py:187
  185.0 9.5 %reduce_sum.95 = f32[8,4,4,32]{0,3,2,1:T(8,128)S(1)} reduce(f32[8,4,4,4,4,32,4]{0,6,5,4,3,2,1:T(4,128)} %bitcast.562, f32[]{:T(128)} %constant.554.clone.1), dimensions={2,4,6}, to_apply=%region_6.7 | reduce | flops 258048 | bytes 1064964 | tf_op jit(solution)/shard_map/reduce_sum | solution.py:188
  195.2 8.6 %copy.100 = f32[8,16,16,128]{0,3,2,1:T(8,128)} copy(f32[8,16,16,128]{3,2,1,0:T(8,128)S(1)} %copy-done.3) | data formatting | bytes 2097152 | tf_op jit(solution)/shard_map/mul | solution.py:187
  203.8 9.5 %reduce_sum.96 = f32[8,4,4,32]{0,3,2,1:T(8,128)S(1)} reduce(f32[8,4,4,4,4,32,4]{0,6,5,4,3,2,1:T(4,128)} %bitcast.563, f32[]{:T(128)} %constant.554.clone.1), dimensions={2,4,6}, to_apply=%region_7.8 | reduce | flops 258048 | bytes 1064964 | tf_op jit(solution)/shard_map/reduce_sum | solution.py:188
  214.0 8.6 %copy.101 = f32[8,16,16,128]{0,3,2,1:T(8,128)} copy(f32[8,16,16,128]{3,2,1,0:T(8,128)S(1)} %copy-done.2) | data formatting | bytes 2097152 | tf_op jit(solution)/shard_map/mul | solution.py:187
  222.5 9.4 %reduce_sum.97 = f32[8,4,4,32]{0,3,2,1:T(8,128)S(1)} reduce(f32[8,4,4,4,4,32,4]{0,6,5,4,3,2,1:T(4,128)} %bitcast.564, f32[]{:T(128)} %constant.554.clone.1), dimensions={2,4,6}, to_apply=%region_8.9 | reduce | flops 258048 | bytes 1064964 | tf_op jit(solution)/shard_map/reduce_sum | solution.py:188
  232.0 8.6 %copy.102 = f32[8,16,16,128]{0,3,2,1:T(8,128)} copy(f32[8,16,16,128]{3,2,1,0:T(8,128)S(1)} %get-tuple-element.33) | data formatting | bytes 2097152 | tf_op jit(solution)/shard_map/mul | solution.py:187
  240.6 9.4 %reduce_sum.98 = f32[8,4,4,32]{0,3,2,1:T(8,128)S(1)} reduce(f32[8,4,4,4,4,32,4]{0,6,5,4,3,2,1:T(4,128)} %bitcast.565, f32[]{:T(128)} %constant.554.clone.1), dimensions={2,4,6}, to_apply=%region_9.10 | reduce | flops 258048 | bytes 1064964 | tf_op jit(solution)/shard_map/reduce_sum | solution.py:188
  250.2 8.6 %copy.103 = f32[8,16,16,128]{0,3,2,1:T(8,128)} copy(f32[8,16,16,128]{3,2,1,0:T(8,128)S(1)} %get-tuple-element.12) | data formatting | bytes 2097152 | tf_op jit(solution)/shard_map/mul | solution.py:187
  258.7 9.4 %reduce_sum.99 = f32[8,4,4,32]{0,3,2,1:T(8,128)S(1)} reduce(f32[8,4,4,4,4,32,4]{0,6,5,4,3,2,1:T(4,128)} %bitcast.566, f32[]{:T(128)} %constant.554.clone.1), dimensions={2,4,6}, to_apply=%region_10.11 | reduce | flops 258048 | bytes 1064964 | tf_op jit(solution)/shard_map/reduce_sum | solution.py:188
  271.6 8.2 %collective-permute-start.18 = (f32[27,1,4,16]{3,2,1,0:T(4,128)S(1)}, f32[27,1,4,16]{3,2,1,0:T(4,128)S(1)}, u32[]{:S(2)}, u32[]{:S(2)}) collective-permute-start(f32[27,1,4,16]{3,2,1,0:T(4,128)S(1)} %get-tuple-element.60), channel_id=1, source_target_pairs={{0,16},{16,32},{32,48},{48,64},{64,80},{80,96},{96,112},{112,128},... | collective-permute-start | bytes 20744 | tf_op jit(solution)/shard_map/ppermute | solution.py:27
  281.9 27.5 %all-reduce.10 = f32[1024]{0:T(1024)S(1)} all-reduce(f32[1024]{0:T(1024)S(1)} %bitcast_dynamic-update-slice_fusion.8), channel_id=2, replica_groups=mesh['gx'=16,'gy'=16] {'gy'}, use_global_device_ids=true, to_apply=%add.10 | all-reduce | flops 1024 | bytes 8192
  324.2 14.9 %all-gather.1 = f32[16,64,27]{1,2,0:T(8,128)S(1)} all-gather(f32[1,64,27]{1,2,0:T(8,128)S(1)} %copy.118), channel_id=1, replica_groups=mesh['gx'=16,'gy'=16] {'gy'}, dimensions={0}, use_global_device_ids=true | all-gather | bytes 117504 | tf_op jit(solution)/shard_map/all_gather | solution.py:203
  (191 shorter events, 104.0 us)
Async XLA Ops:
  1.4 26.2 %collective-permute-start = (s32[6,1,2,16]{3,1,2,0:T(1,128)S(1)}, s32[6,1,2,16]{3,1,2,0:T(1,128)S(1)}, u32[]{:S(2)}, u32[]{:S(2)}) collective-permute-start(s32[6,1,2,16]{3,1,2,0:T(1,128)S(1)} %bitcast.583), channel_id=1, source_target_pairs={{0,16},{16,32},{32,48},{48,64},{64,80},{80,96},{96,112},{112,128},... | collective-permute-start | bytes 2312 | tf_op jit(solution)/shard_map/ppermute | solution.py:27
  7.2 20.4 %collective-permute-start.1 = (s32[6,1,2,16]{3,1,2,0:T(1,128)S(1)}, s32[6,1,2,16]{3,1,2,0:T(1,128)S(1)}, u32[]{:S(2)}, u32[]{:S(2)}) collective-permute-start(s32[6,1,2,16]{3,1,2,0:T(1,128)S(1)} %bitcast.582), channel_id=1, source_target_pairs={{16,0},{32,16},{48,32},{64,48},{80,64},{96,80},{112,96},{128,112},... | collective-permute-start | bytes 2312 | tf_op jit(solution)/shard_map/ppermute | solution.py:30
  9.8 56.5 %collective-permute-start.4 = (f32[1,16,128]{2,1,0:T(8,128)S(1)}, f32[1,16,128]{2,1,0:T(8,128)S(1)}, u32[]{:S(2)}, u32[]{:S(2)}) collective-permute-start(f32[1,16,128]{2,1,0:T(8,128)S(1)} %slice_bitcast_fusion.1), channel_id=1, source_target_pairs={{0,16},{16,32},{32,48},{48,64},{64,80},{80,96},{96,112},{112,128},... | collective-permute-start | bytes 24584 | tf_op jit(solution)/shard_map/ppermute | solution.py:38
  18.2 48.1 %collective-permute-start.5 = (f32[16,1,128]{2,1,0:T(1,128)S(1)}, f32[16,1,128]{2,1,0:T(1,128)S(1)}, u32[]{:S(2)}, u32[]{:S(2)}) collective-permute-start(f32[16,1,128]{2,1,0:T(1,128)S(1)} %slice_bitcast_fusion), channel_id=1, source_target_pairs={{0,1},{1,2},{2,3},{3,4},{4,5},{5,6},{6,7},{7,8},{8,9},{9,10},{10,1... | collective-permute-start | bytes 24584 | tf_op jit(solution)/shard_map/ppermute | solution.py:38
  27.6 4.4 %collective-permute-start.2 = (s32[6,4,1,16]{3,1,2,0:T(4,128)S(1)}, s32[6,4,1,16]{3,1,2,0:T(4,128)S(1)}, u32[]{:S(2)}, u32[]{:S(2)}) collective-permute-start(s32[6,4,1,16]{3,1,2,0:T(4,128)S(1)} %get-tuple-element.71), channel_id=1, source_target_pairs={{0,1},{1,2},{2,3},{3,4},{4,5},{5,6},{6,7},{7,8},{8,9},{9,10},{10,1... | collective-permute-start | bytes 4616 | tf_op jit(solution)/shard_map/ppermute | solution.py:27
  29.5 7.1 %collective-permute-start.3 = (s32[6,4,1,16]{3,1,2,0:T(4,128)S(1)}, s32[6,4,1,16]{3,1,2,0:T(4,128)S(1)}, u32[]{:S(2)}, u32[]{:S(2)}) collective-permute-start(s32[6,4,1,16]{3,1,2,0:T(4,128)S(1)} %get-tuple-element.72), channel_id=1, source_target_pairs={{1,0},{2,1},{3,2},{4,3},{5,4},{6,5},{7,6},{8,7},{9,8},{10,9},{11,1... | collective-permute-start | bytes 4616 | tf_op jit(solution)/shard_map/ppermute | solution.py:30
  47.4 54.9 %copy-start.14 = (u32[256]{0:T(256)S(1)}, u32[256]{0:T(256)}, u32[]{:S(2)}) copy-start(u32[256]{0:T(256)} %constant.586) | copy-start | bytes 3076
  47.6 10.9 %collective-permute-start.6 = (f32[8,1,16,128]{3,2,1,0:T(8,128)S(1)}, f32[8,1,16,128]{3,2,1,0:T(8,128)S(1)}, u32[]{:S(2)}, u32[]{:S(2)}) collective-permute-start(f32[8,1,16,128]{3,2,1,0:T(8,128)S(1)} %get-tuple-element.49), channel_id=1, source_target_pairs={{16,0},{32,16},{48,32},{64,48},{80,64},{96,80},{112,96},{128,112},... | collective-permute-start | bytes 196616 | tf_op jit(solution)/shard_map/ppermute | solution.py:30
  49.5 9.0 %collective-permute-start.7 = (f32[8,1,16,128]{3,2,1,0:T(8,128)S(1)}, f32[8,1,16,128]{3,2,1,0:T(8,128)S(1)}, u32[]{:S(2)}, u32[]{:S(2)}) collective-permute-start(f32[8,1,16,128]{3,2,1,0:T(8,128)S(1)} %get-tuple-element.48), channel_id=1, source_target_pairs={{0,16},{16,32},{32,48},{48,64},{64,80},{80,96},{96,112},{112,128},... | collective-permute-start | bytes 196616 | tf_op jit(solution)/shard_map/ppermute | solution.py:27
  58.6 7.9 %collective-permute-start.8 = (f32[8,18,1,128]{3,2,1,0:T(1,128)S(1)}, f32[8,18,1,128]{3,2,1,0:T(1,128)S(1)}, u32[]{:S(2)}, u32[]{:S(2)}) collective-permute-start(f32[8,18,1,128]{3,2,1,0:T(1,128)S(1)} %get-tuple-element.31), channel_id=1, source_target_pairs={{1,0},{2,1},{3,2},{4,3},{5,4},{6,5},{7,6},{8,7},{9,8},{10,9},{11,1... | collective-permute-start | bytes 221192 | tf_op jit(solution)/shard_map/ppermute | solution.py:30
  60.5 7.1 %collective-permute-start.9 = (f32[8,18,1,128]{3,2,1,0:T(1,128)S(1)}, f32[8,18,1,128]{3,2,1,0:T(1,128)S(1)}, u32[]{:S(2)}, u32[]{:S(2)}) collective-permute-start(f32[8,18,1,128]{3,2,1,0:T(1,128)S(1)} %get-tuple-element.32), channel_id=1, source_target_pairs={{0,1},{1,2},{2,3},{3,4},{4,5},{5,6},{6,7},{7,8},{8,9},{9,10},{10,1... | collective-permute-start | bytes 221192 | tf_op jit(solution)/shard_map/ppermute | solution.py:27
  69.0 10.2 %collective-permute-start.10 = (f32[8,1,16,128]{3,2,1,0:T(8,128)S(1)}, f32[8,1,16,128]{3,2,1,0:T(8,128)S(1)}, u32[]{:S(2)}, u32[]{:S(2)}) collective-permute-start(f32[8,1,16,128]{3,2,1,0:T(8,128)S(1)} %get-tuple-element.45), channel_id=1, source_target_pairs={{16,0},{32,16},{48,32},{64,48},{80,64},{96,80},{112,96},{128,112},... | collective-permute-start | bytes 196616 | tf_op jit(solution)/shard_map/ppermute | solution.py:30
  70.9 9.2 %collective-permute-start.11 = (f32[8,1,16,128]{3,2,1,0:T(8,128)S(1)}, f32[8,1,16,128]{3,2,1,0:T(8,128)S(1)}, u32[]{:S(2)}, u32[]{:S(2)}) collective-permute-start(f32[8,1,16,128]{3,2,1,0:T(8,128)S(1)} %get-tuple-element.44), channel_id=1, source_target_pairs={{0,16},{16,32},{32,48},{48,64},{64,80},{80,96},{96,112},{112,128},... | collective-permute-start | bytes 196616 | tf_op jit(solution)/shard_map/ppermute | solution.py:27
  80.2 9.6 %collective-permute-start.12 = (f32[8,18,1,128]{3,2,1,0:T(1,128)S(1)}, f32[8,18,1,128]{3,2,1,0:T(1,128)S(1)}, u32[]{:S(2)}, u32[]{:S(2)}) collective-permute-start(f32[8,18,1,128]{3,2,1,0:T(1,128)S(1)} %get-tuple-element.29), channel_id=1, source_target_pairs={{1,0},{2,1},{3,2},{4,3},{5,4},{6,5},{7,6},{8,7},{9,8},{10,9},{11,1... | collective-permute-start | bytes 221192 | tf_op jit(solution)/shard_map/ppermute | solution.py:30
  82.1 8.7 %collective-permute-start.13 = (f32[8,18,1,128]{3,2,1,0:T(1,128)S(1)}, f32[8,18,1,128]{3,2,1,0:T(1,128)S(1)}, u32[]{:S(2)}, u32[]{:S(2)}) collective-permute-start(f32[8,18,1,128]{3,2,1,0:T(1,128)S(1)} %get-tuple-element.30), channel_id=1, source_target_pairs={{0,1},{1,2},{2,3},{3,4},{4,5},{5,6},{6,7},{7,8},{8,9},{9,10},{10,1... | collective-permute-start | bytes 221192 | tf_op jit(solution)/shard_map/ppermute | solution.py:27
  92.2 11.4 %collective-permute-start.14 = (f32[8,1,16,128]{3,2,1,0:T(8,128)S(1)}, f32[8,1,16,128]{3,2,1,0:T(8,128)S(1)}, u32[]{:S(2)}, u32[]{:S(2)}) collective-permute-start(f32[8,1,16,128]{3,2,1,0:T(8,128)S(1)} %get-tuple-element.41), channel_id=1, source_target_pairs={{16,0},{32,16},{48,32},{64,48},{80,64},{96,80},{112,96},{128,112},... | collective-permute-start | bytes 196616 | tf_op jit(solution)/shard_map/ppermute | solution.py:30
  94.1 9.5 %collective-permute-start.15 = (f32[8,1,16,128]{3,2,1,0:T(8,128)S(1)}, f32[8,1,16,128]{3,2,1,0:T(8,128)S(1)}, u32[]{:S(2)}, u32[]{:S(2)}) collective-permute-start(f32[8,1,16,128]{3,2,1,0:T(8,128)S(1)} %get-tuple-element.40), channel_id=1, source_target_pairs={{0,16},{16,32},{32,48},{48,64},{64,80},{80,96},{96,112},{112,128},... | collective-permute-start | bytes 196616 | tf_op jit(solution)/shard_map/ppermute | solution.py:27
  103.7 9.5 %collective-permute-start.16 = (f32[8,18,1,128]{3,2,1,0:T(1,128)S(1)}, f32[8,18,1,128]{3,2,1,0:T(1,128)S(1)}, u32[]{:S(2)}, u32[]{:S(2)}) collective-permute-start(f32[8,18,1,128]{3,2,1,0:T(1,128)S(1)} %get-tuple-element.27), channel_id=1, source_target_pairs={{1,0},{2,1},{3,2},{4,3},{5,4},{6,5},{7,6},{8,7},{9,8},{10,9},{11,1... | collective-permute-start | bytes 221192 | tf_op jit(solution)/shard_map/ppermute | solution.py:30
  105.6 8.6 %collective-permute-start.17 = (f32[8,18,1,128]{3,2,1,0:T(1,128)S(1)}, f32[8,18,1,128]{3,2,1,0:T(1,128)S(1)}, u32[]{:S(2)}, u32[]{:S(2)}) collective-permute-start(f32[8,18,1,128]{3,2,1,0:T(1,128)S(1)} %get-tuple-element.28), channel_id=1, source_target_pairs={{0,1},{1,2},{2,3},{3,4},{4,5},{5,6},{6,7},{7,8},{8,9},{9,10},{10,1... | collective-permute-start | bytes 221192 | tf_op jit(solution)/shard_map/ppermute | solution.py:27
  250.2 73.8 %copy-start.12 = (pred[2]{0:T(512)(128)(4,1)S(1)}, pred[2]{0:T(512)(128)(4,1)}, u32[]{:S(2)}) copy-start(pred[2]{0:T(512)(128)(4,1)} %constant.561.clone.1) | copy-start | bytes 10
  271.6 37.8 %collective-permute-start.18 = (f32[27,1,4,16]{3,2,1,0:T(4,128)S(1)}, f32[27,1,4,16]{3,2,1,0:T(4,128)S(1)}, u32[]{:S(2)}, u32[]{:S(2)}) collective-permute-start(f32[27,1,4,16]{3,2,1,0:T(4,128)S(1)} %get-tuple-element.60), channel_id=1, source_target_pairs={{0,16},{16,32},{32,48},{48,64},{64,80},{80,96},{96,112},{112,128},... | collective-permute-start | bytes 20744 | tf_op jit(solution)/shard_map/ppermute | solution.py:27
  279.8 29.6 %collective-permute-start.19 = (f32[27,1,4,16]{3,2,1,0:T(4,128)S(1)}, f32[27,1,4,16]{3,2,1,0:T(4,128)S(1)}, u32[]{:S(2)}, u32[]{:S(2)}) collective-permute-start(f32[27,1,4,16]{3,2,1,0:T(4,128)S(1)} %get-tuple-element.61), channel_id=1, source_target_pairs={{16,0},{32,16},{48,32},{64,48},{80,64},{96,80},{112,96},{128,112},... | collective-permute-start | bytes 20744 | tf_op jit(solution)/shard_map/ppermute | solution.py:30
  309.6 8.8 %collective-permute-start.20 = (f32[27,6,1,16]{3,2,1,0:T(1,128)S(1)}, f32[27,6,1,16]{3,2,1,0:T(1,128)S(1)}, u32[]{:S(2)}, u32[]{:S(2)}) collective-permute-start(f32[27,6,1,16]{3,2,1,0:T(1,128)S(1)} %get-tuple-element.58), channel_id=1, source_target_pairs={{0,1},{1,2},{2,3},{3,4},{4,5},{5,6},{6,7},{7,8},{8,9},{9,10},{10,1... | collective-permute-start | bytes 31112 | tf_op jit(solution)/shard_map/ppermute | solution.py:27
  315.9 7.9 %collective-permute-start.21 = (f32[27,6,1,16]{3,2,1,0:T(1,128)S(1)}, f32[27,6,1,16]{3,2,1,0:T(1,128)S(1)}, u32[]{:S(2)}, u32[]{:S(2)}) collective-permute-start(f32[27,6,1,16]{3,2,1,0:T(1,128)S(1)} %get-tuple-element.59), channel_id=1, source_target_pairs={{1,0},{2,1},{3,2},{4,3},{5,4},{6,5},{7,6},{8,7},{9,8},{10,9},{11,1... | collective-permute-start | bytes 31112 | tf_op jit(solution)/shard_map/ppermute | solution.py:30
  (13 other events, 238.1 us)
where the time goes:
time: 346 us; the launch traced here: 341 us
  starting transfers between devices  97.5 us (28%)
  other arithmetic  94 us (27%)
  local copies, waits for them, and re-layouts  80.1 us (23%)
  blocking collectives  42.4 us (12%)
  waiting for transfers between devices  14.6 us (4%)
  matrix products  9.88 us (3%)
    reduce_sum x8, other arithmetic, on_device(): picked.reshape(8, CX // H, H, CY // H, H, CZ // H, H).sum(axis=(2, 4, 6))  75.4 us
    mul x8, local copies, waits for them, and re-layouts, on_device(): picked = applied * (move_code == move_id)  69.7 us
    ppermute x10, starting transfers between devices, padded_2(): lax.ppermute(lax.slice_in_dim(block, block.shape[dim] - width, None, axis...  66.2 us
    unnamed x1, blocking collectives  27.5 us
    ppermute x10, starting transfers between devices, padded_2(): lax.ppermute(lax.slice_in_dim(block, 0, width, axis=dim), axis, backward)  19.7 us
    all_gather x1, blocking collectives, on_device(): lax.all_gather(rows_dev, 'gy', axis=1, tiled=True)  14.9 us
    ppermute x2, starting transfers between devices, passed_along(): return lax.ppermute(block, axis, route)  11.5 us
    ppermute x10, waiting for transfers between devices, padded_2(): lax.ppermute(lax.slice_in_dim(block, 0, width, axis=dim), axis, backward)  10.4 us
  transfers between devices with their start and end apart: 22, of which 7 were waited for; matrix products, arithmetic and copies ran while one was open for 6% of the time, Pallas kernels for 0%

commit v1 on v0

v1 whole, which is shorter than its diff:
```python
import functools

import jax
import jax.numpy as jnp
from jax import lax
from jax.experimental import pallas as pl
from jax.experimental.pallas import tpu as pltpu
from jax.sharding import PartitionSpec as P

MESH = pl.DeviceIdType.MESH
F32 = jnp.float32
HIGHEST = lax.Precision.HIGHEST

E = 24
FY, FZ, FX, CODE = range(4)
AROUND = [(dx, dy) for dx in (-1, 0, 1) for dy in (-1, 0, 1) if (dx, dy) != (0, 0)]
SUM_START = (-1, 4, 7, 12)
SUM_MASKED = ((0, 1), (3, 4), (0, 1), (3, 4))


def iota(shape, dim):
    return lax.broadcasted_iota(jnp.int32, shape, dim)


def dot(a, b):
    return lax.dot_general(a, b, (((1,), (0,)), ((), ())), precision=HIGHEST, preferred_element_type=F32)


def dot_nt(a, b):
    return lax.dot_general(a, b, (((1,), (1,)), ((), ())), precision=HIGHEST, preferred_element_type=F32)


def kernel(n_x, n_y, ft, pt, sp, ow, pro, rows_out,
           own, rxl, rxh, ypl, yph, ryl, ryh, pd, rp, pe, ex, yz, fe, cf, mk, ba, bb, ap, wm, acc, xs, ct, pp, orow,
           snd, rcv, x_send, x_recv, y_send, y_recv, p_send, p_recv, e_send, e_recv):
    gx = lax.axis_index("gx")
    gy = lax.axis_index("gy")
    peer = lambda dx, dy: (lax.rem(gx + (dx + n_x), n_x), lax.rem(gy + (dy + n_y), n_y))

    barrier = pltpu.get_barrier_semaphore()
    far = [j for j in range(1, n_y) if j not in (1, n_y - 1)]
    for dx, dy in AROUND:
        pl.semaphore_signal(barrier, inc=1, device_id=peer(dx, dy), device_id_type=MESH)
    for j in far:
        pl.semaphore_signal(barrier, inc=1, device_id=peer(0, j), device_id_type=MESH)

    pd[...] = jnp.zeros((8, 128), F32)
    for bx in range(2):
        total = None
        for k in range(6):
            place = (iota((16, 128), 1) == iota((16, 128), 0) + 16 * k).astype(F32)
            term = dot(sp[k, bx].astype(F32), place)
            total = term if total is None else total + term
        pd[2 * bx:2 * bx + 2, :] = total

    x_last = gx == n_x - 1
    y_last = gy == n_y - 1
    row16 = iota((16, 128), 0)
    lane16 = iota((16, 128), 1)
    keep_y = jnp.where((row16 == 15) & y_last, 0.0, 1.0)
    keep_z = jnp.where(lane16 == 127, 0.0, 1.0)

    def stage(x, carry):
        keep_x = jnp.where((x == 15) & x_last, 0.0, 1.0)
        p = pt[x]
        px = (p >= 9).astype(jnp.int32) + (p >= 18).astype(jnp.int32)
        q = p - 9 * px
        py = (q >= 3).astype(jnp.int32) + (q >= 6).astype(jnp.int32)
        pz = q - 3 * py
        bx = ((x >> 3) + px + 1) & 1
        by = ((row16 >> 3) + py + 1) & 1
        bz = ((lane16 >> 3) + pz + 1) & 1
        code = (4 * bx + 2 * by + bz).astype(F32)
        values = {FX: ft[0, x] * keep_x, FY: ft[1, x] * keep_y, FZ: ft[2, x] * keep_z, CODE: code}
        for k in range(4):
            own[x * 4 + k] = values[k]
            fe[k, x + 4, 12:28, :] = values[k]
            start = pl.multiple_of(x * 16, 8) + 4 * k
            ypl[pl.ds(start, 4), :] = values[k][0:4]
            yph[pl.ds(start, 4), :] = values[k][12:16]
        return carry

    lax.fori_loop(0, 16, stage, 0)
    pl.semaphore_wait(barrier, 8 + len(far))

    def remote(src, dst, send, recv, dx, dy):
        copy = pltpu.make_async_remote_copy(src_ref=src, dst_ref=dst, send_sem=send, recv_sem=recv,
                                            device_id=peer(dx, dy), device_id_type=MESH)
        copy.start()
        return copy

    pad_copies = [
        remote(pd, rp.at[pl.ds(8 * d, 8)], p_send.at[d], p_recv.at[d], dx, dy) for d, (dx, dy) in enumerate(AROUND)
    ]
    halo = [
        remote(own.at[pl.ds(50, 14)], rxl, x_send.at[0], x_recv.at[0], 1, 0),
        remote(own.at[pl.ds(0, 12)], rxh.at[pl.ds(0, 12)], x_send.at[1], x_recv.at[1], -1, 0),
        remote(own.at[pl.ds(15, 1)], rxh.at[pl.ds(12, 1)], x_send.at[2], x_recv.at[2], -1, 0),
        remote(yph, ryl.at[pl.ds(64, 256)], y_send.at[0], y_recv.at[0], 0, 1),
        remote(ypl, ryh.at[pl.ds(64, 256)], y_send.at[1], y_recv.at[1], 0, -1),
        remote(yph.at[pl.ds(192, 64)], ryl.at[pl.ds(0, 64)], y_send.at[2], y_recv.at[2], 1, 1),
        remote(yph.at[pl.ds(0, 64)], ryl.at[pl.ds(320, 64)], y_send.at[3], y_recv.at[3], -1, 1),
        remote(ypl.at[pl.ds(192, 64)], ryh.at[pl.ds(0, 64)], y_send.at[4], y_recv.at[4], 1, -1),
        remote(ypl.at[pl.ds(0, 64)], ryh.at[pl.ds(320, 64)], y_send.at[5], y_recv.at[5], -1, -1),
    ]

    zero8 = jnp.zeros((8, 128), F32)

    def clear(x, carry):
        for s in range(8):
            for b in (ba, bb):
                b[s, x, 0:8, :] = zero8
                b[s, x, 32:40, :] = zero8
        for k in range(4):
            fe[k, x, 0:8, :] = zero8
        return carry

    lax.fori_loop(0, E, clear, 0)

    orow[...] = jnp.full((8, 128), -1.0, F32)
    orow[0:1, 0:64] = ow[...].astype(F32)
    owner = jnp.broadcast_to(orow[0:1, :], (128, 128))
    earlier = (owner == owner.T) & (iota((128, 128), 0) < iota((128, 128), 1))
    rank = jnp.sum(earlier.astype(F32), axis=0, keepdims=True)
    target = orow[0:1, :] * 8.0 + rank
    row_f = iota((128, 128), 0).astype(F32)
    for b in range(4):
        shifted = jnp.broadcast_to(target, (8, 128))
        if b:
            shifted = pltpu.roll(shifted, 128 - 16 * b, 1)
        pp[b] = ((row_f == shifted[0:1]) & (iota((128, 128), 1) < 16)).astype(F32)

    c = iota((128, 256), 1)
    up_z, b_x, up_x, b_y, up_y = c >> 7, (c >> 6) & 1, (c >> 5) & 1, (c >> 4) & 1, (c >> 3) & 1
    s_x, s_y, s_z = (c >> 2) & 1, (c >> 1) & 1, c & 1
    o_x = jnp.where(s_x == b_x, 1, 2 * up_x)
    o_y = jnp.where(s_y == b_y, 1, 2 * up_y)
    o_z = jnp.where(s_z == 0, 1, 2 * up_z)
    ct[...] = (iota((128, 256), 0) == (b_x * 2 + b_y) * 32 + 9 * o_x + 3 * o_y + o_z).astype(F32)

    for copy in pad_copies:
        copy.wait_recv()
    low = {-1: 0, 0: 1, 1: 3}
    for dx, dy in AROUND + [(0, 0)]:
        sx, sy = -dx, -dy
        base = 0 if (dx, dy) == (0, 0) else 8 * AROUND.index((dx, dy))
        src = pd if (dx, dy) == (0, 0) else rp
        for i in ((1,) if sx < 0 else (0,) if sx > 0 else (0, 1)):
            for j in ((1,) if sy < 0 else (0,) if sy > 0 else (0, 1)):
                bi = low[sx] + (i if sx == 0 else 0)
                bj = low[sy] + (j if sy == 0 else 0)
                pe[4 * bi + bj:4 * bi + bj + 1, :] = src[base + 2 * i + j:base + 2 * i + j + 1, :]
    block_row = iota((16, 128), 0)
    outside = ((((block_row >> 2) == 0) & (gx == 0)) | (((block_row >> 2) == 3) & x_last)
               | (((block_row & 3) == 0) & (gy == 0)) | (((block_row & 3) == 3) & y_last))
    pads = jnp.where(outside, 0.0, pe[...])
    r_in = iota((128, 128), 0)
    tile_z = (iota((128, 128), 1) + 4) >> 3
    for sz in range(2):
        upper = (tile_z & 1) == sz
        bz = jnp.where(upper, tile_z, tile_z - 1)
        fits = (bz >= 0) & (bz < 16)
        for k in range(5):
            lanes = bz + 16 * k if k < 4 else bz + jnp.where(upper, 64, 80)
            ex[sz * 5 + k] = dot(pads, (fits & (r_in == lanes)).astype(F32))

    row8 = iota((8, 128), 0).astype(F32)
    lane8 = iota((8, 128), 1)
    i_z = ((lane8 + 4) & 7).astype(F32)
    up8 = ((lane8 + 4) >> 3) & 1
    for s in range(8):
        sx, sy, sz = s >> 2, (s >> 1) & 1, s & 1
        for g in range(3):
            bx = g if g % 2 == sx else g - 1
            for t in range(3):
                by = t if t % 2 == sy else t - 1
                r = (bx + 1) * 4 + by + 1
                reach_z = ex[sz * 5 + 4, r:r + 1, :]
                ok_z = jnp.where(up8 == sz, i_z + reach_z, 7.0 - i_z + reach_z) >= 4.0
                if by == t:
                    ok_y = row8 + ex[sz * 5 + 2, r:r + 1, :] >= 4.0
                else:
                    ok_y = row8 <= 3.0 + ex[sz * 5 + 3, r:r + 1, :]
                yz[s, g, 8 * t:8 * t + 8, :] = (ok_z & ok_y).astype(F32)

    def masks(i, carry):
        at = i.astype(F32)
        for s in range(8):
            sx, sy, sz = s >> 2, (s >> 1) & 1, s & 1
            for g in range(3):
                bx = g if g % 2 == sx else g - 1
                for t in range(3):
                    by = t if t % 2 == sy else t - 1
                    r = (bx + 1) * 4 + by + 1
                    if bx == g:
                        ok_x = ex[sz * 5, r:r + 1, :] >= 4.0 - at
                    else:
                        ok_x = ex[sz * 5 + 1, r:r + 1, :] >= at - 3.0
                    mk[s, 8 * g + i, 8 * t:8 * t + 8, :] = jnp.where(ok_x, yz[s, g, 8 * t:8 * t + 8, :], 0.0)
        return carry

    lax.fori_loop(0, 8, masks, 0)

    for copy in halo:
        copy.wait_recv()

    for i in range(14):
        flat = 50 + i
        fe[flat % 4, flat // 4 - 12, 12:28, :] = rxl[i]
    for i in range(12):
        fe[i % 4, 20 + i // 4, 12:28, :] = rxh[i]
    fe[CODE, 23, 12:28, :] = rxh[12]

    def unpack(x, carry):
        for k in range(4):
            start = pl.multiple_of(x * 16, 8) + 4 * k
            fe[k, x, 8:12, :] = ryl[pl.ds(start, 4), :]
            fe[k, x, 28:32, :] = ryh[pl.ds(start, 4), :]
        return carry

    lax.fori_loop(0, E, unpack, 0)

    def first(x, carry):
        for t in range(3):
            code = fe[CODE, x, 8 + 8 * t:16 + 8 * t, :]
            for s in range(8):
                ba[s, x, 8 + 8 * t:16 + 8 * t, :] = (code == float(s)).astype(F32)
        return carry

    lax.fori_loop(0, E, first, 0)

    def coefficients(x, carry):
        for t in range(3):
            a, b = 8 + 8 * t, 16 + 8 * t
            east, west = fe[FX, x, a:b, :], fe[FX, x - 1, a:b, :]
            north, south = fe[FY, x, a:b, :], fe[FY, x, a - 1:b - 1, :]
            top = fe[FZ, x, a:b, :]
            bottom = pltpu.roll(top, 1, 1)
            diagonal = west + east + south + north + bottom + top
            inverse = 1.0 / diagonal
            for i, face in enumerate((east, west, north, south, top, bottom)):
                cf[i, x, 8 * t:8 * t + 8, :] = face * inverse
            cf[6, x, 8 * t:8 * t + 8, :] = diagonal
        return carry

    lax.fori_loop(1, E - 1, coefficients, 0)

    def around(src, s, x, t, faces):
        east, west, north, south, top, bottom = faces
        a, b = 8 + 8 * t, 16 + 8 * t
        centre = src[s, x, a:b, :]
        total = (east * src[s, x + 1, a:b, :] + west * src[s, x - 1, a:b, :]
                 + north * src[s, x, a + 1:b + 1, :] + south * src[s, x, a - 1:b - 1, :]
                 + top * pltpu.roll(centre, 127, 1) + bottom * pltpu.roll(centre, 1, 1))
        return centre, total

    def smooth(src, dst, x, carry):
        for t in range(3):
            faces = [cf[i, x, 8 * t:8 * t + 8, :] for i in range(6)]
            updated = []
            for s in range(8):
                centre, total = around(src, s, x, t, faces)
                updated.append(mk[s, x, 8 * t:8 * t + 8, :] * (0.5 * centre + total))
            whole = ((updated[0] + updated[1]) + (updated[2] + updated[3])) + (
                (updated[4] + updated[5]) + (updated[6] + updated[7]))
            scale = 1.0 / jnp.where(whole > 0.0, whole, 1.0)
            for s in range(8):
                dst[s, x, 8 + 8 * t:16 + 8 * t, :] = updated[s] * scale
        return carry

    lax.fori_loop(1, E - 1, functools.partial(smooth, ba, bb), 0)
    lax.fori_loop(2, E - 2, functools.partial(smooth, bb, ba), 0)

    def give(x, carry):
        for s in range(8):
            pro[s, x] = ba[s, x + 4, 12:28, :]
        return carry

    lax.fori_loop(0, 16, give, 0)

    def apply(x, carry):
        for t in range(3):
            faces = [cf[i, x, 8 * t:8 * t + 8, :] for i in range(6)]
            diagonal = cf[6, x, 8 * t:8 * t + 8, :]
            for s in range(8):
                centre, total = around(ba, s, x, t, faces)
                ap[s, x, 8 * t:8 * t + 8, :] = diagonal * (centre - total)
        return carry

    lax.fori_loop(3, E - 3, apply, 0)

    for a in range(4):
        for i in range(5):
            x = SUM_START[a] + 4 + i
            for t in range(3):
                code = fe[CODE, x, 8 + 8 * t:16 + 8 * t, :].astype(jnp.int32)
                in_x = (((code >> 2) & 1) == a // 2).astype(F32)
                odd_y = ((code >> 1) & 1).astype(F32)
                odd_z = (code & 1).astype(F32)
                in_y = 1.0 - odd_y if t == 0 else odd_y
                wm[a * 5 + i, 0, 8 * t:8 * t + 8, :] = in_x
                wm[a * 5 + i, 1, 8 * t:8 * t + 8, :] = in_x * odd_z
                wm[a * 5 + i, 2, 8 * t:8 * t + 8, :] = in_x * in_y
                wm[a * 5 + i, 3, 8 * t:8 * t + 8, :] = in_x * in_y * odd_z

    def sums(s, carry):
        for a in range(4):
            for t in range(3):
                parts = [None] * 4
                for i in range(5):
                    value = ap[s, SUM_START[a] + 4 + i, 8 * t:8 * t + 8, :]
                    for m in range(4) if t == 1 else (2, 3):
                        if m == 0 and i not in SUM_MASKED[a]:
                            term = value
                        else:
                            term = value * wm[a * 5 + i, m, 8 * t:8 * t + 8, :]
                        parts[m] = term if parts[m] is None else parts[m] + term
                for m in range(4) if t == 1 else (2, 3):
                    place = a * 8 + (m - 2 if t == 0 else m + 2 if t == 1 else m + 4)
                    acc[pl.ds(pl.multiple_of((place * 8 + s) * 8, 8), 8), :] = parts[m]
        return carry

    lax.fori_loop(0, 8, sums, 0)

    def over_rows(place):
        total = acc[pl.ds(place * 64, 8, stride=8), :]
        for y in range(1, 8):
            total = total + acc[pl.ds(place * 64 + y, 8, stride=8), :]
        return total

    for a in range(4):
        r = [over_rows(a * 8 + m) for m in range(8)]
        r[2], r[3] = r[2] - r[4], r[3] - r[5]
        for b in range(4):
            for m in range(2):
                start = m * 128 + (a * 4 + b) * 8
                xs[start:start + 8, :] = r[2 * b + m]

    lane_tile = (iota((128, 128), 0) + 4) >> 3
    col = iota((128, 128), 1)
    even = (col & 1) == 0
    even_row = (iota((128, 128), 0) & 1) == 0
    halves = []
    for up in range(2):
        gather = ((lane_tile == col + up) & (col < 16)).astype(F32)
        z = dot(xs[...], gather)
        v = jnp.where(even, z[0:128] - z[128:256], z[128:256])
        other = jnp.where(even_row, pltpu.roll(v, 127, 0), pltpu.roll(v, 1, 0))
        halves.append(jnp.where(even, v, other))
    entries = dot(ct[:, 0:128], halves[0]) + dot(ct[:, 128:256], halves[1])
    routed = dot_nt(pp[0], entries[0:32])
    for b in range(1, 4):
        routed = routed + dot_nt(pp[b], entries[32 * b:32 * b + 32])
    snd[:, 0:32] = routed
    snd[:, 32:128] = jnp.zeros((128, 96), F32)

    mine = pl.multiple_of(gy * 8, 8)
    sent = []
    for j in range(1, n_y):
        there = lax.rem(gy + j, n_y)
        sent.append(remote(snd.at[pl.ds(pl.multiple_of(there * 8, 8), 8)], rcv.at[pl.ds(mine, 8)],
                           e_send.at[j], e_recv.at[j], 0, j))
    rcv[pl.ds(mine, 8), :] = snd[pl.ds(mine, 8), :]
    for copy in sent:
        copy.wait_recv()
    rows_out[...] = rcv[...].T[0:27, :]
    for copy in pad_copies + halo + sent:
        copy.wait_send()


def solution(mesh):
    n_x, n_y = mesh.shape["gx"], mesh.shape["gy"]
    vmem = pl.BlockSpec(memory_space=pltpu.VMEM)
    dma = pltpu.SemaphoreType.DMA

    def on_device(face_trans, partition, support_pad, owners):
        prolongation, rows = pl.pallas_call(
            functools.partial(kernel, n_x, n_y),
            out_shape=(
                jax.ShapeDtypeStruct((8, 16, 16, 128), F32),
                jax.ShapeDtypeStruct((27, 128), F32),
            ),
            in_specs=[vmem] * 4,
            out_specs=(vmem, vmem),
            scratch_shapes=[
                pltpu.VMEM((64, 16, 128), F32),
                pltpu.VMEM((14, 16, 128), F32),
                pltpu.VMEM((13, 16, 128), F32),
                pltpu.VMEM((256, 128), F32),
                pltpu.VMEM((256, 128), F32),
                pltpu.VMEM((384, 128), F32),
                pltpu.VMEM((384, 128), F32),
                pltpu.VMEM((8, 128), F32),
                pltpu.VMEM((64, 128), F32),
                pltpu.VMEM((16, 128), F32),
                pltpu.VMEM((10, 16, 128), F32),
                pltpu.VMEM((8, 3, E, 128), F32),
                pltpu.VMEM((4, E, 40, 128), F32),
                pltpu.VMEM((7, E, E, 128), F32),
                pltpu.VMEM((8, E, E, 128), F32),
                pltpu.VMEM((8, E, 40, 128), F32),
                pltpu.VMEM((8, E, 40, 128), F32),
                pltpu.VMEM((8, E, E, 128), F32),
                pltpu.VMEM((20, 4, E, 128), F32),
                pltpu.VMEM((2048, 128), F32),
                pltpu.VMEM((256, 128), F32),
                pltpu.VMEM((128, 256), F32),
                pltpu.VMEM((4, 128, 128), F32),
                pltpu.VMEM((8, 128), F32),
                pltpu.VMEM((128, 128), F32),
                pltpu.VMEM((8 * n_y, 128), F32),
                dma((3,)), dma((3,)), dma((6,)), dma((6,)), dma((8,)), dma((8,)), dma((n_y,)), dma((n_y,)),
            ],
            compiler_params=pltpu.CompilerParams(
                collective_id=0, has_side_effects=True, vmem_limit_bytes=48 * 2**20
            ),
        )(face_trans, partition, support_pad, owners.reshape(1, 64))
        return prolongation, rows.reshape(1, 1, 27, 128)

    placed = (
        P(None, "gx", "gy", None),
        P("gx", "gy", None),
        P(None, "gx", "gy", None),
        P("gx", "gy", None, None),
    )
    return jax.shard_map(
        on_device,
        mesh=mesh,
        in_specs=placed,
        out_specs=(P(None, "gx", "gy", None), P("gx", "gy", None, None)),
        check_vma=False,
    )
```

time: 346 us -> 47.4 us (0.14)
  the two profiles are of different devices: /device:TPU:95 before, /device:TPU:1 now
where the time goes in v1:
time: 47.4 us; the launch traced here: 47.2 us
  Pallas kernels  41.7 us (88%)
  local copies, waits for them, and re-layouts  4.84 us (10%)
  between operations  0.65 us (1%)
    pallas_call x1, Pallas kernels, on_device(): pl.pallas_call(functools.partial(kernel, n_x, n_y), out_shape=(jax.ShapeD...  41.7 us
    unnamed x10, local copies, waits for them, and re-layouts  4.84 us

profile of v1, /device:TPU:1, one launch (start us, length us, event | category | flops | bytes accessed | tf_op | source)
XLA Modules:
  0.0 47.2 jit_solution(10189419558941538169)
XLA Ops:
  0.6 0.0 copy-start.3
  0.6 0.6 %copy-done.3 = s32[1,1,64,1]{2,3,1,0:T(1,128)S(1)} copy-done((s32[1,1,64,1]{2,3,1,0:T(1,128)S(1)}, s32[1,1,64,1]{2,3,1,0:T(1,128)}, u32[]{:S(2)}) %copy-start.3) | copy-done | bytes 280
  1.3 0.0 copy-start
  1.3 1.0 %copy-done = f32[3,16,16,128]{3,2,1,0:T(8,128)S(1)} copy-done((f32[3,16,16,128]{3,2,1,0:T(8,128)S(1)}, f32[3,16,16,128]{3,2,1,0:T(8,128)}, u32[]{:S(2)}) %copy-start) | copy-done | bytes 393240
  2.3 0.0 copy-start.1
  2.3 0.9 %copy-done.1 = s32[16,16,128]{2,1,0:T(8,128)S(1)} copy-done((s32[16,16,128]{2,1,0:T(8,128)S(1)}, s32[16,16,128]{2,1,0:T(8,128)}, u32[]{:S(2)}) %copy-start.1) | copy-done | bytes 131096
  3.2 0.0 copy-start.2
  3.2 0.7 %copy-done.2 = s32[6,2,2,16]{3,2,1,0:T(2,128)S(1)} copy-done((s32[6,2,2,16]{3,2,1,0:T(2,128)S(1)}, s32[6,2,2,16]{3,2,1,0:T(2,128)}, u32[]{:S(2)}) %copy-start.2) | copy-done | bytes 1560
  3.9 41.7 %shard_map.59 = (f32[8,16,16,128]{3,2,1,0:T(8,128)S(1)}, f32[27,128]{1,0:T(8,128)S(1)}) custom-call(f32[3,16,16,128]{3,2,1,0:T(8,128)S(1)} %copy-done, s32[16,16,128]{2,1,0:T(8,128)S(1)} %copy-done.1, s32[6,2,2,16]{3,2,1,0:T(2,128)S(1)} %copy-done.2, s32[1,64]{1,0:T(1,128)S(1)} %bitcast.3), custom_call_target="tpu_custom_call" | custom-call | tf_op jit(solution)/shard_map/pallas_call | solution.py:377
  45.6 0.6 %copy.6 = f32[1,1,27,128]{3,1,2,0:T(1,128)} copy(f32[1,1,27,128]{3,2,1,0:T(8,128)S(1)} %bitcast.2) | data formatting | bytes 27648
  46.3 1.0 %copy.8 = f32[8,16,16,128]{3,2,1,0:T(8,128)} copy(f32[8,16,16,128]{3,2,1,0:T(8,128)S(1)} %get-tuple-element.10) | data formatting | bytes 2097152
Async XLA Ops:
  0.6 0.7 %copy-start.3 = (s32[1,1,64,1]{2,3,1,0:T(1,128)S(1)}, s32[1,1,64,1]{2,3,1,0:T(1,128)}, u32[]{:S(2)}) copy-start(s32[1,1,64,1]{2,3,1,0:T(1,128)} %param.7) | copy-start | bytes 772
  1.3 1.0 %copy-start = (f32[3,16,16,128]{3,2,1,0:T(8,128)S(1)}, f32[3,16,16,128]{3,2,1,0:T(8,128)}, u32[]{:S(2)}) copy-start(f32[3,16,16,128]{3,2,1,0:T(8,128)} %ft.1) | copy-start | bytes 1179652
  2.3 0.9 %copy-start.1 = (s32[16,16,128]{2,1,0:T(8,128)S(1)}, s32[16,16,128]{2,1,0:T(8,128)}, u32[]{:S(2)}) copy-start(s32[16,16,128]{2,1,0:T(8,128)} %pt.1) | copy-start | bytes 393220
  3.2 0.7 %copy-start.2 = (s32[6,2,2,16]{3,2,1,0:T(2,128)S(1)}, s32[6,2,2,16]{3,2,1,0:T(2,128)}, u32[]{:S(2)}) copy-start(s32[6,2,2,16]{3,2,1,0:T(2,128)} %sp.1) | copy-start | bytes 4612

commit v2 on v1

--- a/solution.py
+++ b/solution.py
@@ -30,9 +30,9 @@
     return lax.dot_general(a, b, (((1,), (1,)), ((), ())), precision=HIGHEST, preferred_element_type=F32)
 
 
-def kernel(n_x, n_y, ft, pt, sp, ow, pro, rows_out,
-           own, rxl, rxh, ypl, yph, ryl, ryh, pd, rp, pe, ex, yz, fe, cf, mk, ba, bb, ap, wm, acc, xs, ct, pp, orow,
-           snd, rcv, x_send, x_recv, y_send, y_recv, p_send, p_recv, e_send, e_recv):
+def kernel(n_x, n_y, ft_in, pt_in, sp_in, ow_in, pro_out, rows_out,
+           ft, pt, sp, ow, pro, rows, own, rxl, rxh, ypl, yph, ryl, ryh, pd, rp, pe, ex, yz, fe, cf, mk, ba, bb, ap, wm, acc, xs, ct, pp, orow,
+           snd, rcv, in_sem, out_sem, x_send, x_recv, y_send, y_recv, p_send, p_recv, e_send, e_recv):
     gx = lax.axis_index("gx")
     gy = lax.axis_index("gy")
     peer = lambda dx, dy: (lax.rem(gx + (dx + n_x), n_x), lax.rem(gy + (dy + n_y), n_y))
@@ -43,6 +43,28 @@
         pl.semaphore_signal(barrier, inc=1, device_id=peer(dx, dy), device_id_type=MESH)
     for j in far:
         pl.semaphore_signal(barrier, inc=1, device_id=peer(0, j), device_id_type=MESH)
+
+    loads = [
+        pltpu.make_async_copy(src, dst, in_sem.at[i])
+        for i, (src, dst) in enumerate(((ft_in, ft), (pt_in, pt), (sp_in, sp), (ow_in, ow)))
+    ]
+    for copy in loads:
+        copy.start()
+
+    zero8 = jnp.zeros((8, 128), F32)
+
+    def clear(x, carry):
+        for s in range(8):
+            for b in (ba, bb):
+                b[s, x, 0:8, :] = zero8
+                b[s, x, 32:40, :] = zero8
+        for k in range(4):
+            fe[k, x, 0:8, :] = zero8
+        return carry
+
+    lax.fori_loop(0, E, clear, 0)
+    for copy in loads:
+        copy.wait()
 
     pd[...] = jnp.zeros((8, 128), F32)
     for bx in range(2):
@@ -92,30 +114,19 @@
     pad_copies = [
         remote(pd, rp.at[pl.ds(8 * d, 8)], p_send.at[d], p_recv.at[d], dx, dy) for d, (dx, dy) in enumerate(AROUND)
     ]
-    halo = [
+    y_copies = [
+        remote(yph, ryl.at[pl.ds(64, 256)], y_send.at[0], y_recv.at[0], 0, 1),
+        remote(ypl, ryh.at[pl.ds(64, 256)], y_send.at[1], y_recv.at[1], 0, -1),
+    ]
+    x_copies = [
         remote(own.at[pl.ds(50, 14)], rxl, x_send.at[0], x_recv.at[0], 1, 0),
         remote(own.at[pl.ds(0, 12)], rxh.at[pl.ds(0, 12)], x_send.at[1], x_recv.at[1], -1, 0),
         remote(own.at[pl.ds(15, 1)], rxh.at[pl.ds(12, 1)], x_send.at[2], x_recv.at[2], -1, 0),
-        remote(yph, ryl.at[pl.ds(64, 256)], y_send.at[0], y_recv.at[0], 0, 1),
-        remote(ypl, ryh.at[pl.ds(64, 256)], y_send.at[1], y_recv.at[1], 0, -1),
         remote(yph.at[pl.ds(192, 64)], ryl.at[pl.ds(0, 64)], y_send.at[2], y_recv.at[2], 1, 1),
         remote(yph.at[pl.ds(0, 64)], ryl.at[pl.ds(320, 64)], y_send.at[3], y_recv.at[3], -1, 1),
         remote(ypl.at[pl.ds(192, 64)], ryh.at[pl.ds(0, 64)], y_send.at[4], y_recv.at[4], 1, -1),
         remote(ypl.at[pl.ds(0, 64)], ryh.at[pl.ds(320, 64)], y_send.at[5], y_recv.at[5], -1, -1),
     ]
-
-    zero8 = jnp.zeros((8, 128), F32)
-
-    def clear(x, carry):
-        for s in range(8):
-            for b in (ba, bb):
-                b[s, x, 0:8, :] = zero8
-                b[s, x, 32:40, :] = zero8
-        for k in range(4):
-            fe[k, x, 0:8, :] = zero8
-        return carry
-
-    lax.fori_loop(0, E, clear, 0)
 
     orow[...] = jnp.full((8, 128), -1.0, F32)
     orow[0:1, 0:64] = ow[...].astype(F32)
@@ -199,37 +210,26 @@
                     mk[s, 8 * g + i, 8 * t:8 * t + 8, :] = jnp.where(ok_x, yz[s, g, 8 * t:8 * t + 8, :], 0.0)
         return carry
 
-    lax.fori_loop(0, 8, masks, 0)
-
-    for copy in halo:
+    lax.fori_loop(0, 8, masks, 0, unroll=4)
+
+    for copy in y_copies:
         copy.wait_recv()
 
-    for i in range(14):
-        flat = 50 + i
-        fe[flat % 4, flat // 4 - 12, 12:28, :] = rxl[i]
-    for i in range(12):
-        fe[i % 4, 20 + i // 4, 12:28, :] = rxh[i]
-    fe[CODE, 23, 12:28, :] = rxh[12]
-
-    def unpack(x, carry):
+    def unpack(x):
         for k in range(4):
-            start = pl.multiple_of(x * 16, 8) + 4 * k
+            start = 16 * x + 4 * k
+            if not isinstance(x, int):
+                start = pl.multiple_of(x * 16, 8) + 4 * k
             fe[k, x, 8:12, :] = ryl[pl.ds(start, 4), :]
             fe[k, x, 28:32, :] = ryh[pl.ds(start, 4), :]
-        return carry
-
-    lax.fori_loop(0, E, unpack, 0)
-
-    def first(x, carry):
+
+    def first(x):
         for t in range(3):
             code = fe[CODE, x, 8 + 8 * t:16 + 8 * t, :]
             for s in range(8):
                 ba[s, x, 8 + 8 * t:16 + 8 * t, :] = (code == float(s)).astype(F32)
-        return carry
-
-    lax.fori_loop(0, E, first, 0)
-
-    def coefficients(x, carry):
+
+    def coefficients(x):
         for t in range(3):
             a, b = 8 + 8 * t, 16 + 8 * t
             east, west = fe[FX, x, a:b, :], fe[FX, x - 1, a:b, :]
@@ -241,9 +241,6 @@
             for i, face in enumerate((east, west, north, south, top, bottom)):
                 cf[i, x, 8 * t:8 * t + 8, :] = face * inverse
             cf[6, x, 8 * t:8 * t + 8, :] = diagonal
-        return carry
-
-    lax.fori_loop(1, E - 1, coefficients, 0)
 
     def around(src, s, x, t, faces):
         east, west, north, south, top, bottom = faces
@@ -254,7 +251,7 @@
                  + top * pltpu.roll(centre, 127, 1) + bottom * pltpu.roll(centre, 1, 1))
         return centre, total
 
-    def smooth(src, dst, x, carry):
+    def smooth(src, dst, x):
         for t in range(3):
             faces = [cf[i, x, 8 * t:8 * t + 8, :] for i in range(6)]
             updated = []
@@ -266,30 +263,16 @@
             scale = 1.0 / jnp.where(whole > 0.0, whole, 1.0)
             for s in range(8):
                 dst[s, x, 8 + 8 * t:16 + 8 * t, :] = updated[s] * scale
-        return carry
-
-    lax.fori_loop(1, E - 1, functools.partial(smooth, ba, bb), 0)
-    lax.fori_loop(2, E - 2, functools.partial(smooth, bb, ba), 0)
-
-    def give(x, carry):
-        for s in range(8):
-            pro[s, x] = ba[s, x + 4, 12:28, :]
-        return carry
-
-    lax.fori_loop(0, 16, give, 0)
-
-    def apply(x, carry):
+
+    def apply(x):
         for t in range(3):
             faces = [cf[i, x, 8 * t:8 * t + 8, :] for i in range(6)]
             diagonal = cf[6, x, 8 * t:8 * t + 8, :]
             for s in range(8):
                 centre, total = around(ba, s, x, t, faces)
                 ap[s, x, 8 * t:8 * t + 8, :] = diagonal * (centre - total)
-        return carry
-
-    lax.fori_loop(3, E - 3, apply, 0)
-
-    for a in range(4):
+
+    def weigh(a):
         for i in range(5):
             x = SUM_START[a] + 4 + i
             for t in range(3):
@@ -303,38 +286,94 @@
                 wm[a * 5 + i, 2, 8 * t:8 * t + 8, :] = in_x * in_y
                 wm[a * 5 + i, 3, 8 * t:8 * t + 8, :] = in_x * in_y * odd_z
 
-    def sums(s, carry):
-        for a in range(4):
-            for t in range(3):
-                parts = [None] * 4
-                for i in range(5):
-                    value = ap[s, SUM_START[a] + 4 + i, 8 * t:8 * t + 8, :]
-                    for m in range(4) if t == 1 else (2, 3):
-                        if m == 0 and i not in SUM_MASKED[a]:
-                            term = value
-                        else:
-                            term = value * wm[a * 5 + i, m, 8 * t:8 * t + 8, :]
-                        parts[m] = term if parts[m] is None else parts[m] + term
+    def sums(a, s):
+        for t in range(3):
+            parts = [None] * 4
+            for i in range(5):
+                value = ap[s, SUM_START[a] + 4 + i, 8 * t:8 * t + 8, :]
                 for m in range(4) if t == 1 else (2, 3):
-                    place = a * 8 + (m - 2 if t == 0 else m + 2 if t == 1 else m + 4)
-                    acc[pl.ds(pl.multiple_of((place * 8 + s) * 8, 8), 8), :] = parts[m]
-        return carry
-
-    lax.fori_loop(0, 8, sums, 0)
-
-    def over_rows(place):
-        total = acc[pl.ds(place * 64, 8, stride=8), :]
-        for y in range(1, 8):
-            total = total + acc[pl.ds(place * 64 + y, 8, stride=8), :]
-        return total
-
-    for a in range(4):
-        r = [over_rows(a * 8 + m) for m in range(8)]
+                    if m == 0 and i not in SUM_MASKED[a]:
+                        term = value
+                    else:
+                        term = value * wm[a * 5 + i, m, 8 * t:8 * t + 8, :]
+                    parts[m] = term if parts[m] is None else parts[m] + term
+            for m in range(4) if t == 1 else (2, 3):
+                place = a * 8 + (m - 2 if t == 0 else m + 2 if t == 1 else m + 4)
+                acc[pl.ds(pl.multiple_of((place * 8 + s) * 8, 8), 8), :] = parts[m]
+
+    def over_rows(a):
+        r = []
+        for place in range(a * 8, a * 8 + 8):
+            total = acc[pl.ds(place * 64, 8, stride=8), :]
+            for y in range(1, 8):
+                total = total + acc[pl.ds(place * 64 + y, 8, stride=8), :]
+            r.append(total)
         r[2], r[3] = r[2] - r[4], r[3] - r[5]
         for b in range(4):
             for m in range(2):
                 start = m * 128 + (a * 4 + b) * 8
                 xs[start:start + 8, :] = r[2 * b + m]
+
+    def layers(step, start, stop, unroll):
+        def body(x, carry):
+            step(x)
+            return carry
+
+        lax.fori_loop(start, stop, body, 0, unroll=unroll)
+
+    def both(step, start, other, count, unroll):
+        def body(i, carry):
+            step(start + i)
+            step(other + i)
+            return carry
+
+        lax.fori_loop(0, count, body, 0, unroll=unroll)
+
+    def give(x):
+        for s in range(8):
+            pro[s, x] = ba[s, x + 4, 12:28, :]
+
+    once = functools.partial(smooth, ba, bb)
+    twice = functools.partial(smooth, bb, ba)
+
+    layers(unpack, 4, 20, 8)
+    layers(first, 4, 20, 8)
+    layers(coefficients, 5, 20, 5)
+    layers(once, 5, 19, 7)
+    layers(twice, 6, 18, 6)
+    layers(give, 2, 14, 4)
+    layers(apply, 7, 17, 5)
+    weigh(1)
+    weigh(2)
+    layers(functools.partial(sums, 1), 0, 8, 4)
+    layers(functools.partial(sums, 2), 0, 8, 4)
+
+    for copy in x_copies:
+        copy.wait_recv()
+    for i in range(14):
+        flat = 50 + i
+        fe[flat % 4, flat // 4 - 12, 12:28, :] = rxl[i]
+    for i in range(12):
+        fe[i % 4, 20 + i // 4, 12:28, :] = rxh[i]
+    fe[CODE, 23, 12:28, :] = rxh[12]
+    for x in range(4):
+        unpack(x)
+        unpack(20 + x)
+    both(first, 0, 20, 4, 4)
+    layers(coefficients, 1, 5, 4)
+    layers(coefficients, 20, 23, 3)
+    both(once, 1, 19, 4, 4)
+    both(twice, 2, 18, 4, 4)
+    both(give, 0, 14, 2, 2)
+    write = pltpu.make_async_copy(pro, pro_out, out_sem.at[0])
+    write.start()
+    both(apply, 3, 17, 4, 4)
+    weigh(0)
+    weigh(3)
+    layers(functools.partial(sums, 0), 0, 8, 4)
+    layers(functools.partial(sums, 3), 0, 8, 4)
+    for a in range(4):
+        over_rows(a)
 
     lane_tile = (iota((128, 128), 0) + 4) >> 3
     col = iota((128, 128), 1)
@@ -363,14 +402,18 @@
     rcv[pl.ds(mine, 8), :] = snd[pl.ds(mine, 8), :]
     for copy in sent:
         copy.wait_recv()
-    rows_out[...] = rcv[...].T[0:27, :]
-    for copy in pad_copies + halo + sent:
+    rows[...] = rcv[...].T[0:27, :]
+    write_rows = pltpu.make_async_copy(rows, rows_out, out_sem.at[1])
+    write_rows.start()
+    write.wait()
+    write_rows.wait()
+    for copy in pad_copies + y_copies + x_copies + sent:
         copy.wait_send()
 
 
 def solution(mesh):
     n_x, n_y = mesh.shape["gx"], mesh.shape["gy"]
-    vmem = pl.BlockSpec(memory_space=pltpu.VMEM)
+    hbm = pl.BlockSpec(memory_space=pltpu.HBM)
     dma = pltpu.SemaphoreType.DMA
 
     def on_device(face_trans, partition, support_pad, owners):
@@ -380,9 +423,15 @@
                 jax.ShapeDtypeStruct((8, 16, 16, 128), F32),
                 jax.ShapeDtypeStruct((27, 128), F32),
             ),
-            in_specs=[vmem] * 4,
-            out_specs=(vmem, vmem),
+            in_specs=[hbm] * 4,
+            out_specs=(hbm, hbm),
             scratch_shapes=[
+                pltpu.VMEM((3, 16, 16, 128), F32),
+                pltpu.VMEM((16, 16, 128), jnp.int32),
+                pltpu.VMEM((6, 2, 2, 16), jnp.int32),
+                pltpu.VMEM((1, 64), jnp.int32),
+                pltpu.VMEM((8, 16, 16, 128), F32),
+                pltpu.VMEM((27, 128), F32),
                 pltpu.VMEM((64, 16, 128), F32),
                 pltpu.VMEM((14, 16, 128), F32),
                 pltpu.VMEM((13, 16, 128), F32),
@@ -409,10 +458,10 @@
                 pltpu.VMEM((8, 128), F32),
                 pltpu.VMEM((128, 128), F32),
                 pltpu.VMEM((8 * n_y, 128), F32),
-                dma((3,)), dma((3,)), dma((6,)), dma((6,)), dma((8,)), dma((8,)), dma((n_y,)), dma((n_y,)),
+                dma((4,)), dma((2,)), dma((3,)), dma((3,)), dma((6,)), dma((6,)), dma((8,)), dma((8,)), dma((n_y,)), dma((n_y,)),
             ],
             compiler_params=pltpu.CompilerParams(
-                collective_id=0, has_side_effects=True, vmem_limit_bytes=48 * 2**20
+                collective_id=0, has_side_effects=True, vmem_limit_bytes=60 * 2**20
             ),
         )(face_trans, partition, support_pad, owners.reshape(1, 64))
         return prolongation, rows.reshape(1, 1, 27, 128)

time: 47.4 us -> 37.5 us (0.79)
  Pallas kernels: 41.7 us -> 33.1 us
  local copies, waits for them, and re-layouts: 4.84 us -> 3.6 us
    pallas_call x1, Pallas kernels: 41.7 us -> 33.1 us  [on_device(): pl.pallas_call(functools.partial(kernel, n_x, n_y), out_shape=(jax.ShapeD...]
    unnamed x10 -> x2, local copies, waits for them, and re-layouts: 4.84 us -> 3.6 us
where the time goes in v2:
time: 37.5 us; the launch traced here: 37.3 us
  Pallas kernels  33.1 us (88%)
  local copies, waits for them, and re-layouts  3.6 us (10%)
  between operations  0.64 us (2%)
    pallas_call x1, Pallas kernels, on_device(): pl.pallas_call(functools.partial(kernel, n_x, n_y), out_shape=(jax.ShapeD...  33.1 us
    unnamed x2, local copies, waits for them, and re-layouts  3.6 us

profile of v2, /device:TPU:1, one launch (start us, length us, event | category | flops | bytes accessed | tf_op | source)
XLA Modules:
  0.0 37.3 jit_solution(3799789550225836660)
XLA Ops:
  0.6 33.1 %shard_map.59 = (f32[8,16,16,128]{3,2,1,0:T(8,128)}, f32[27,128]{1,0:T(8,128)}) custom-call(f32[3,16,16,128]{3,2,1,0:T(8,128)} %ft_in.1, s32[16,16,128]{2,1,0:T(8,128)} %pt_in.1, s32[6,2,2,16]{3,2,1,0:T(2,128)} %sp_in.1, s32[1,64]{1,0:T(1,128)} %bitcast.3), custom_call_target="tpu_custom_call" | custom-call | tf_op jit(solution)/shard_map/pallas_call | solution.py:420
  33.7 1.3 %copy.6 = f32[1,1,27,128]{3,1,2,0:T(1,128)} copy(f32[1,1,27,128]{3,2,1,0:T(8,128)} %bitcast.2) | data formatting | bytes 27648
  35.0 2.3 %copy.8 = f32[8,16,16,128]{3,2,1,0:T(8,128)} copy(f32[8,16,16,128]{3,2,1,0:T(8,128)} %get-tuple-element.10) | data formatting | bytes 2097152

commit v3 on v2

--- a/solution.py
+++ b/solution.py
@@ -30,17 +30,32 @@
     return lax.dot_general(a, b, (((1,), (1,)), ((), ())), precision=HIGHEST, preferred_element_type=F32)
 
 
-def kernel(n_x, n_y, ft_in, pt_in, sp_in, ow_in, pro_out, rows_out,
-           ft, pt, sp, ow, pro, rows, own, rxl, rxh, ypl, yph, ryl, ryh, pd, rp, pe, ex, yz, fe, cf, mk, ba, bb, ap, wm, acc, xs, ct, pp, orow,
-           snd, rcv, in_sem, out_sem, x_send, x_recv, y_send, y_recv, p_send, p_recv, e_send, e_recv):
+def kernel(n_x, n_y, ft_in, pt_in, sp_in, ow_in, pro, rows,
+           ft, pt, sp, ow, own, rxl, rxh, ypl, yph, ryl, ryh, pd, rp, pe, ex, yz, fe, cf, mk, ba, bb, ap, wm, acc, xs, ct, pp, orow,
+           snd, rcv, in_sem, x_send, x_recv, y_send, y_recv, p_send, p_recv, e_send, e_recv):
     gx = lax.axis_index("gx")
     gy = lax.axis_index("gy")
     peer = lambda dx, dy: (lax.rem(gx + (dx + n_x), n_x), lax.rem(gy + (dy + n_y), n_y))
 
     barrier = pltpu.get_barrier_semaphore()
     far = [j for j in range(1, n_y) if j not in (1, n_y - 1)]
+
+    def inside(dx, dy):
+        fits = None
+        for d, at, count in ((dx, gx, n_x), (dy, gy, n_y)):
+            if d:
+                part = at > 0 if d < 0 else at < count - 1
+                fits = part if fits is None else fits & part
+        return fits
+
     for dx, dy in AROUND:
-        pl.semaphore_signal(barrier, inc=1, device_id=peer(dx, dy), device_id_type=MESH)
+        def greet(dx=dx, dy=dy):
+            pl.semaphore_signal(barrier, inc=1, device_id=peer(dx, dy), device_id_type=MESH)
+
+        if dx == 0:
+            greet()
+        else:
+            pl.when(inside(dx, dy))(greet)
     for j in far:
         pl.semaphore_signal(barrier, inc=1, device_id=peer(0, j), device_id_type=MESH)
 
@@ -103,30 +118,87 @@
         return carry
 
     lax.fori_loop(0, 16, stage, 0)
-    pl.semaphore_wait(barrier, 8 + len(far))
+    sides_x = 2 - (gx == 0).astype(jnp.int32) - x_last.astype(jnp.int32)
+    sides_y = 2 - (gy == 0).astype(jnp.int32) - y_last.astype(jnp.int32)
+    pl.semaphore_wait(barrier, 2 + len(far) + sides_x * (1 + sides_y))
 
     def remote(src, dst, send, recv, dx, dy):
-        copy = pltpu.make_async_remote_copy(src_ref=src, dst_ref=dst, send_sem=send, recv_sem=recv,
+        return pltpu.make_async_remote_copy(src_ref=src, dst_ref=dst, send_sem=send, recv_sem=recv,
                                             device_id=peer(dx, dy), device_id_type=MESH)
-        copy.start()
-        return copy
+
+    def between(act, copies, sign=1):
+        for (dx, dy), copy in copies:
+            pl.when(inside(sign * dx, sign * dy))(functools.partial(act, copy))
+
+    def start(copies):
+        between(lambda copy: copy.start(), copies)
+
+    def arrive(copies):
+        between(lambda copy: copy.wait_recv(), copies, -1)
+
+    def leave(copies):
+        between(lambda copy: copy.wait_send(), copies)
+
+    def link(src, dst, send, recv, dx, dy):
+        return (dx, dy), remote(src, dst, send, recv, dx, dy)
 
     pad_copies = [
-        remote(pd, rp.at[pl.ds(8 * d, 8)], p_send.at[d], p_recv.at[d], dx, dy) for d, (dx, dy) in enumerate(AROUND)
+        link(pd, rp.at[pl.ds(8 * d, 8)], p_send.at[d], p_recv.at[d], dx, dy) for d, (dx, dy) in enumerate(AROUND)
     ]
     y_copies = [
-        remote(yph, ryl.at[pl.ds(64, 256)], y_send.at[0], y_recv.at[0], 0, 1),
-        remote(ypl, ryh.at[pl.ds(64, 256)], y_send.at[1], y_recv.at[1], 0, -1),
+        link(yph, ryl.at[pl.ds(64, 256)], y_send.at[0], y_recv.at[0], 0, 1),
+        link(ypl, ryh.at[pl.ds(64, 256)], y_send.at[1], y_recv.at[1], 0, -1),
     ]
     x_copies = [
-        remote(own.at[pl.ds(50, 14)], rxl, x_send.at[0], x_recv.at[0], 1, 0),
-        remote(own.at[pl.ds(0, 12)], rxh.at[pl.ds(0, 12)], x_send.at[1], x_recv.at[1], -1, 0),
-        remote(own.at[pl.ds(15, 1)], rxh.at[pl.ds(12, 1)], x_send.at[2], x_recv.at[2], -1, 0),
-        remote(yph.at[pl.ds(192, 64)], ryl.at[pl.ds(0, 64)], y_send.at[2], y_recv.at[2], 1, 1),
-        remote(yph.at[pl.ds(0, 64)], ryl.at[pl.ds(320, 64)], y_send.at[3], y_recv.at[3], -1, 1),
-        remote(ypl.at[pl.ds(192, 64)], ryh.at[pl.ds(0, 64)], y_send.at[4], y_recv.at[4], 1, -1),
-        remote(ypl.at[pl.ds(0, 64)], ryh.at[pl.ds(320, 64)], y_send.at[5], y_recv.at[5], -1, -1),
+        link(own.at[pl.ds(50, 14)], rxl, x_send.at[0], x_recv.at[0], 1, 0),
+        link(own.at[pl.ds(0, 12)], rxh.at[pl.ds(0, 12)], x_send.at[1], x_recv.at[1], -1, 0),
+        link(own.at[pl.ds(15, 1)], rxh.at[pl.ds(12, 1)], x_send.at[2], x_recv.at[2], -1, 0),
+        link(yph.at[pl.ds(192, 64)], ryl.at[pl.ds(0, 64)], y_send.at[2], y_recv.at[2], 1, 1),
+        link(yph.at[pl.ds(0, 64)], ryl.at[pl.ds(320, 64)], y_send.at[3], y_recv.at[3], -1, 1),
+        link(ypl.at[pl.ds(192, 64)], ryh.at[pl.ds(0, 64)], y_send.at[4], y_recv.at[4], 1, -1),
+        link(ypl.at[pl.ds(0, 64)], ryh.at[pl.ds(320, 64)], y_send.at[5], y_recv.at[5], -1, -1),
     ]
+
+    start(x_copies[:3])
+    start(pad_copies)
+    start(y_copies)
+    start(x_copies[3:])
+
+    def beyond(ref, layers_of_x, code):
+        for x in layers_of_x:
+            ref[16 * x:16 * x + 16, :] = jnp.ones((16, 128), F32)
+            ref[16 * x + 4 * CODE:16 * x + 4 * CODE + 4, :] = jnp.full((4, 128), code, F32)
+
+    def closed_west():
+        for r in (ryl, ryh):
+            r[48 + 4 * FX:52 + 4 * FX, :] = jnp.zeros((4, 128), F32)
+
+    @pl.when(gx == 0)
+    def _():
+        for i in range(14):
+            k = (50 + i) % 4
+            rxl[i] = jnp.full((16, 128), 6.0 if k == CODE else 0.0 if (k, i) == (FX, 12) else 1.0, F32)
+        beyond(ryl, range(4), 6.0)
+        beyond(ryh, range(4), 6.0)
+        closed_west()
+
+    @pl.when(x_last)
+    def _():
+        rxh[...] = jnp.ones_like(rxh)
+        beyond(ryl, range(20, 24), 1.0)
+        beyond(ryh, range(20, 24), 1.0)
+
+    @pl.when(gy == 0)
+    def _():
+        beyond(ryl, range(E), 6.0)
+        for x in range(E):
+            ryl[16 * x + 4 * FY + 3:16 * x + 4 * FY + 4, :] = jnp.zeros((1, 128), F32)
+        pl.when(gx == 0)(closed_west)
+
+    @pl.when(y_last)
+    def _():
+        beyond(ryh, range(E), 1.0)
+        pl.when(gx == 0)(closed_west)
 
     orow[...] = jnp.full((8, 128), -1.0, F32)
     orow[0:1, 0:64] = ow[...].astype(F32)
@@ -149,8 +221,7 @@
     o_z = jnp.where(s_z == 0, 1, 2 * up_z)
     ct[...] = (iota((128, 256), 0) == (b_x * 2 + b_y) * 32 + 9 * o_x + 3 * o_y + o_z).astype(F32)
 
-    for copy in pad_copies:
-        copy.wait_recv()
+    arrive(pad_copies)
     low = {-1: 0, 0: 1, 1: 3}
     for dx, dy in AROUND + [(0, 0)]:
         sx, sy = -dx, -dy
@@ -212,8 +283,7 @@
 
     lax.fori_loop(0, 8, masks, 0, unroll=4)
 
-    for copy in y_copies:
-        copy.wait_recv()
+    arrive(y_copies)
 
     def unpack(x):
         for k in range(4):
@@ -348,8 +418,7 @@
     layers(functools.partial(sums, 1), 0, 8, 4)
     layers(functools.partial(sums, 2), 0, 8, 4)
 
-    for copy in x_copies:
-        copy.wait_recv()
+    arrive(x_copies)
     for i in range(14):
         flat = 50 + i
         fe[flat % 4, flat // 4 - 12, 12:28, :] = rxl[i]
@@ -365,8 +434,6 @@
     both(once, 1, 19, 4, 4)
     both(twice, 2, 18, 4, 4)
     both(give, 0, 14, 2, 2)
-    write = pltpu.make_async_copy(pro, pro_out, out_sem.at[0])
-    write.start()
     both(apply, 3, 17, 4, 4)
     weigh(0)
     weigh(3)
@@ -397,41 +464,47 @@
     sent = []
     for j in range(1, n_y):
         there = lax.rem(gy + j, n_y)
-        sent.append(remote(snd.at[pl.ds(pl.multiple_of(there * 8, 8), 8)], rcv.at[pl.ds(mine, 8)],
-                           e_send.at[j], e_recv.at[j], 0, j))
+        copy = remote(snd.at[pl.ds(pl.multiple_of(there * 8, 8), 8)], rcv.at[pl.ds(mine, 8)],
+                      e_send.at[j], e_recv.at[j], 0, j)
+        copy.start()
+        sent.append(copy)
     rcv[pl.ds(mine, 8), :] = snd[pl.ds(mine, 8), :]
     for copy in sent:
         copy.wait_recv()
-    rows[...] = rcv[...].T[0:27, :]
-    write_rows = pltpu.make_async_copy(rows, rows_out, out_sem.at[1])
-    write_rows.start()
-    write.wait()
-    write_rows.wait()
-    for copy in pad_copies + y_copies + x_copies + sent:
+    rows[:, 0, :] = rcv[...].T[0:27, :]
+    leave(pad_copies + y_copies + x_copies)
+    for copy in sent:
         copy.wait_send()
+
+
+def writer(pro, rows, pro_out, rows_out, sem):
+    copies = [pltpu.make_async_copy(pro, pro_out, sem.at[0]), pltpu.make_async_copy(rows, rows_out, sem.at[1])]
+    for copy in copies:
+        copy.start()
+    for copy in copies:
+        copy.wait()
 
 
 def solution(mesh):
     n_x, n_y = mesh.shape["gx"], mesh.shape["gy"]
     hbm = pl.BlockSpec(memory_space=pltpu.HBM)
+    vmem = pl.BlockSpec(memory_space=pltpu.VMEM)
     dma = pltpu.SemaphoreType.DMA
 
     def on_device(face_trans, partition, support_pad, owners):
         prolongation, rows = pl.pallas_call(
             functools.partial(kernel, n_x, n_y),
             out_shape=(
-                jax.ShapeDtypeStruct((8, 16, 16, 128), F32),
-                jax.ShapeDtypeStruct((27, 128), F32),
+                pltpu.VMEM((8, 16, 16, 128), F32),
+                pltpu.VMEM((27, 1, 128), F32),
             ),
             in_specs=[hbm] * 4,
-            out_specs=(hbm, hbm),
+            out_specs=(vmem, vmem),
             scratch_shapes=[
                 pltpu.VMEM((3, 16, 16, 128), F32),
                 pltpu.VMEM((16, 16, 128), jnp.int32),
                 pltpu.VMEM((6, 2, 2, 16), jnp.int32),
                 pltpu.VMEM((1, 64), jnp.int32),
-                pltpu.VMEM((8, 16, 16, 128), F32),
-                pltpu.VMEM((27, 128), F32),
                 pltpu.VMEM((64, 16, 128), F32),
                 pltpu.VMEM((14, 16, 128), F32),
                 pltpu.VMEM((13, 16, 128), F32),
@@ -458,12 +531,23 @@
                 pltpu.VMEM((8, 128), F32),
                 pltpu.VMEM((128, 128), F32),
                 pltpu.VMEM((8 * n_y, 128), F32),
-                dma((4,)), dma((2,)), dma((3,)), dma((3,)), dma((6,)), dma((6,)), dma((8,)), dma((8,)), dma((n_y,)), dma((n_y,)),
+                dma((4,)), dma((3,)), dma((3,)), dma((6,)), dma((6,)), dma((8,)), dma((8,)), dma((n_y,)), dma((n_y,)),
             ],
             compiler_params=pltpu.CompilerParams(
-                collective_id=0, has_side_effects=True, vmem_limit_bytes=60 * 2**20
+                collective_id=0, has_side_effects=True, vmem_limit_bytes=48 * 2**20
             ),
-        )(face_trans, partition, support_pad, owners.reshape(1, 64))
+        )(*(pltpu.with_memory_space_constraint(a, pltpu.HBM)
+            for a in (face_trans, partition, support_pad, owners.reshape(1, 64))))
+        prolongation, rows = pl.pallas_call(
+            writer,
+            out_shape=(
+                jax.ShapeDtypeStruct((8, 16, 16, 128), F32),
+                jax.ShapeDtypeStruct((27, 1, 128), F32),
+            ),
+            in_specs=[vmem] * 2,
+            out_specs=(hbm, hbm),
+            scratch_shapes=[dma((2,))],
+        )(*(pltpu.with_memory_space_constraint(a, pltpu.VMEM) for a in (prolongation, rows)))
         return prolongation, rows.reshape(1, 1, 27, 128)
 
     placed = (

time: 37.5 us -> 30.6 us (0.82)
  the two profiles are of different devices: /device:TPU:1 before, /device:TPU:161 now
where the time goes in v3:
time: 30.6 us; the launch traced here: 30.5 us
  Pallas kernels  29.9 us (98%)
  between operations  0.64 us (2%)
    pallas_call x1, Pallas kernels, on_device(): pl.pallas_call(functools.partial(kernel, n_x, n_y), out_shape=(pltpu.VMEM...  28.9 us
    pallas_call x1, Pallas kernels, on_device(): pl.pallas_call(writer, out_shape=(jax.ShapeDtypeStruct((8, 16, 16, 128),...  0.99 us

profile of v3, /device:TPU:161, one launch (start us, length us, event | category | flops | bytes accessed | tf_op | source)
XLA Modules:
  0.0 30.5 jit_solution(14199770341258642341)
XLA Ops:
  0.6 28.9 %shard_map.59 = (f32[8,16,16,128]{3,2,1,0:T(8,128)S(1)}, f32[27,1,128]{2,1,0:T(1,128)S(1)}) custom-call(f32[3,16,16,128]{3,2,1,0:T(8,128)} %ft_in.1, s32[16,16,128]{2,1,0:T(8,128)} %pt_in.1, s32[6,2,2,16]{3,2,1,0:T(2,128)} %sp_in.1, s32[1,64]{1,0:T(1,128)} %bitcast.4), custom_call_target="tpu_custom_call" | custom-call | tf_op jit(solution)/shard_map/pallas_call | solution.py:495
  29.5 1.0 %shard_map.60 = (f32[8,16,16,128]{3,2,1,0:T(8,128)}, f32[27,1,128]{2,1,0:T(1,128)}) custom-call(f32[8,16,16,128]{3,2,1,0:T(8,128)S(1)} %get-tuple-element.6.pro, f32[27,1,128]{2,1,0:T(1,128)S(1)} %get-tuple-element.7.rows), custom_call_target="tpu_custom_call" | custom-call | tf_op jit(solution)/shard_map/pallas_call | solution.py:541

commit v4 on v3

--- a/solution.py
+++ b/solution.py
@@ -149,20 +149,30 @@
         link(yph, ryl.at[pl.ds(64, 256)], y_send.at[0], y_recv.at[0], 0, 1),
         link(ypl, ryh.at[pl.ds(64, 256)], y_send.at[1], y_recv.at[1], 0, -1),
     ]
-    x_copies = [
-        link(own.at[pl.ds(50, 14)], rxl, x_send.at[0], x_recv.at[0], 1, 0),
-        link(own.at[pl.ds(0, 12)], rxh.at[pl.ds(0, 12)], x_send.at[1], x_recv.at[1], -1, 0),
-        link(own.at[pl.ds(15, 1)], rxh.at[pl.ds(12, 1)], x_send.at[2], x_recv.at[2], -1, 0),
-        link(yph.at[pl.ds(192, 64)], ryl.at[pl.ds(0, 64)], y_send.at[2], y_recv.at[2], 1, 1),
-        link(yph.at[pl.ds(0, 64)], ryl.at[pl.ds(320, 64)], y_send.at[3], y_recv.at[3], -1, 1),
-        link(ypl.at[pl.ds(192, 64)], ryh.at[pl.ds(0, 64)], y_send.at[4], y_recv.at[4], 1, -1),
-        link(ypl.at[pl.ds(0, 64)], ryh.at[pl.ds(320, 64)], y_send.at[5], y_recv.at[5], -1, -1),
+    near_copies = [
+        link(own.at[pl.ds(56, 8)], rxl.at[pl.ds(6, 8)], x_send.at[0], x_recv.at[0], 1, 0),
+        link(own.at[pl.ds(0, 8)], rxh.at[pl.ds(0, 8)], x_send.at[1], x_recv.at[1], -1, 0),
     ]
-
-    start(x_copies[:3])
+    deep_copies = [
+        link(own.at[pl.ds(50, 6)], rxl.at[pl.ds(0, 6)], x_send.at[2], x_recv.at[2], 1, 0),
+        link(own.at[pl.ds(8, 4)], rxh.at[pl.ds(8, 4)], x_send.at[3], x_recv.at[3], -1, 0),
+        link(own.at[pl.ds(15, 1)], rxh.at[pl.ds(12, 1)], x_send.at[4], x_recv.at[4], -1, 0),
+    ]
+    near_corners, deep_corners = [], []
+    for corners, from_low, to_low, from_high, to_high in (
+            (near_corners, 224, 32, 0, 320), (deep_corners, 192, 0, 32, 352)):
+        for src, dst, dy in ((yph, ryl, 1), (ypl, ryh, -1)):
+            for dx, a, b in ((1, from_low, to_low), (-1, from_high, to_high)):
+                at = 2 + len(near_corners) + len(deep_corners)
+                corners.append(link(src.at[pl.ds(a, 32)], dst.at[pl.ds(b, 32)], y_send.at[at], y_recv.at[at], dx, dy))
+    start(near_copies)
     start(pad_copies)
     start(y_copies)
-    start(x_copies[3:])
+    start(near_corners)
+    start(deep_copies)
+    start(deep_corners)
+    near_copies += near_corners
+    deep_copies += deep_corners
 
     def beyond(ref, layers_of_x, code):
         for x in layers_of_x:
@@ -418,25 +428,36 @@
     layers(functools.partial(sums, 1), 0, 8, 4)
     layers(functools.partial(sums, 2), 0, 8, 4)
 
-    arrive(x_copies)
-    for i in range(14):
+    arrive(near_copies)
+    for i in range(8):
+        fe[i % 4, 2 + i // 4, 12:28, :] = rxl[6 + i]
+        fe[i % 4, 20 + i // 4, 12:28, :] = rxh[i]
+    for x in (2, 3, 20, 21):
+        unpack(x)
+    both(first, 2, 20, 2, 2)
+    both(coefficients, 3, 20, 2, 2)
+    both(once, 3, 19, 2, 2)
+    both(twice, 4, 18, 2, 2)
+    both(give, 0, 14, 2, 2)
+    both(apply, 5, 17, 2, 2)
+    weigh(0)
+    weigh(3)
+
+    arrive(deep_copies)
+    for i in range(6):
         flat = 50 + i
         fe[flat % 4, flat // 4 - 12, 12:28, :] = rxl[i]
-    for i in range(12):
-        fe[i % 4, 20 + i // 4, 12:28, :] = rxh[i]
+    for i in range(4):
+        fe[i, 22, 12:28, :] = rxh[8 + i]
     fe[CODE, 23, 12:28, :] = rxh[12]
-    for x in range(4):
+    for x in (0, 1, 22, 23):
         unpack(x)
-        unpack(20 + x)
-    both(first, 0, 20, 4, 4)
-    layers(coefficients, 1, 5, 4)
-    layers(coefficients, 20, 23, 3)
-    both(once, 1, 19, 4, 4)
-    both(twice, 2, 18, 4, 4)
-    both(give, 0, 14, 2, 2)
-    both(apply, 3, 17, 4, 4)
-    weigh(0)
-    weigh(3)
+    both(first, 0, 22, 2, 2)
+    both(coefficients, 1, 22, 1, 1)
+    coefficients(2)
+    both(once, 1, 21, 2, 2)
+    both(twice, 2, 20, 2, 2)
+    both(apply, 3, 19, 2, 2)
     layers(functools.partial(sums, 0), 0, 8, 4)
     layers(functools.partial(sums, 3), 0, 8, 4)
     for a in range(4):
@@ -472,7 +493,7 @@
     for copy in sent:
         copy.wait_recv()
     rows[:, 0, :] = rcv[...].T[0:27, :]
-    leave(pad_copies + y_copies + x_copies)
+    leave(pad_copies + y_copies + near_copies + deep_copies)
     for copy in sent:
         copy.wait_send()
 
@@ -531,7 +552,7 @@
                 pltpu.VMEM((8, 128), F32),
                 pltpu.VMEM((128, 128), F32),
                 pltpu.VMEM((8 * n_y, 128), F32),
-                dma((4,)), dma((3,)), dma((3,)), dma((6,)), dma((6,)), dma((8,)), dma((8,)), dma((n_y,)), dma((n_y,)),
+                dma((4,)), dma((5,)), dma((5,)), dma((10,)), dma((10,)), dma((8,)), dma((8,)), dma((n_y,)), dma((n_y,)),
             ],
             compiler_params=pltpu.CompilerParams(
                 collective_id=0, has_side_effects=True, vmem_limit_bytes=48 * 2**20

time: 30.6 us -> 29.6 us (0.967)
  the two profiles are of different devices: /device:TPU:161 before, /device:TPU:95 now
where the time goes in v4:
time: 29.6 us; the launch traced here: 29.5 us
  Pallas kernels  28.9 us (98%)
  between operations  0.64 us (2%)
    pallas_call x1, Pallas kernels, on_device(): pl.pallas_call(functools.partial(kernel, n_x, n_y), out_shape=(pltpu.VMEM...  27.9 us
    pallas_call x1, Pallas kernels, on_device(): pl.pallas_call(writer, out_shape=(jax.ShapeDtypeStruct((8, 16, 16, 128),...  0.99 us

profile of v4, /device:TPU:95, one launch (start us, length us, event | category | flops | bytes accessed | tf_op | source)
XLA Modules:
  0.0 29.5 jit_solution(11799751833095570585)
XLA Ops:
  0.6 27.9 %shard_map.59 = (f32[8,16,16,128]{3,2,1,0:T(8,128)S(1)}, f32[27,1,128]{2,1,0:T(1,128)S(1)}) custom-call(f32[3,16,16,128]{3,2,1,0:T(8,128)} %ft_in.1, s32[16,16,128]{2,1,0:T(8,128)} %pt_in.1, s32[6,2,2,16]{3,2,1,0:T(2,128)} %sp_in.1, s32[1,64]{1,0:T(1,128)} %bitcast.4), custom_call_target="tpu_custom_call" | custom-call | tf_op jit(solution)/shard_map/pallas_call | solution.py:516
  28.5 1.0 %shard_map.60 = (f32[8,16,16,128]{3,2,1,0:T(8,128)}, f32[27,1,128]{2,1,0:T(1,128)}) custom-call(f32[8,16,16,128]{3,2,1,0:T(8,128)S(1)} %get-tuple-element.6.pro, f32[27,1,128]{2,1,0:T(1,128)S(1)} %get-tuple-element.7.rows), custom_call_target="tpu_custom_call" | custom-call | tf_op jit(solution)/shard_map/pallas_call | solution.py:562

commit v5 on v4

--- a/solution.py
+++ b/solution.py
@@ -9,11 +9,11 @@
 
 MESH = pl.DeviceIdType.MESH
 F32 = jnp.float32
-HIGHEST = lax.Precision.HIGHEST
 
 E = 24
 FY, FZ, FX, CODE = range(4)
 AROUND = [(dx, dy) for dx in (-1, 0, 1) for dy in (-1, 0, 1) if (dx, dy) != (0, 0)]
+CORNERS = [(dx, dy) for dx in (1, -1) for dy in (1, -1)]
 SUM_START = (-1, 4, 7, 12)
 SUM_MASKED = ((0, 1), (3, 4), (0, 1), (3, 4))
 
@@ -22,16 +22,37 @@
     return lax.broadcasted_iota(jnp.int32, shape, dim)
 
 
-def dot(a, b):
-    return lax.dot_general(a, b, (((1,), (0,)), ((), ())), precision=HIGHEST, preferred_element_type=F32)
+def parts(a):
+    high = a.astype(jnp.bfloat16)
+    rest = a - high.astype(F32)
+    middle = rest.astype(jnp.bfloat16)
+    return high, middle, (rest - middle.astype(F32)).astype(jnp.bfloat16)
+
+
+def dot(a, b, dims=(((1,), (0,)), ((), ()))):
+    total = None
+    exact = a.astype(jnp.bfloat16)
+    for part in parts(b):
+        term = lax.dot_general(exact, part, dims, preferred_element_type=F32)
+        total = term if total is None else total + term
+    return total
+
+
+def dot_left(a, b):
+    total = None
+    exact = b.astype(jnp.bfloat16)
+    for part in parts(a):
+        term = lax.dot_general(part, exact, (((1,), (0,)), ((), ())), preferred_element_type=F32)
+        total = term if total is None else total + term
+    return total
 
 
 def dot_nt(a, b):
-    return lax.dot_general(a, b, (((1,), (1,)), ((), ())), precision=HIGHEST, preferred_element_type=F32)
+    return dot(a, b, (((1,), (1,)), ((), ())))
 
 
 def kernel(n_x, n_y, ft_in, pt_in, sp_in, ow_in, pro, rows,
-           ft, pt, sp, ow, own, rxl, rxh, ypl, yph, ryl, ryh, pd, rp, pe, ex, yz, fe, cf, mk, ba, bb, ap, wm, acc, xs, ct, pp, orow,
+           ft, pt, sp, ow, own, rxl, rxh, ypl, yph, ryl, ryh, cpk, crx, pd, rp, pe, ex, yz, fe, cf, mk, ba, bb, ap, wm, acc, xs, ct, pp, orow,
            snd, rcv, in_sem, x_send, x_recv, y_send, y_recv, p_send, p_recv, e_send, e_recv):
     gx = lax.axis_index("gx")
     gy = lax.axis_index("gy")
@@ -78,6 +99,12 @@
         return carry
 
     lax.fori_loop(0, E, clear, 0)
+    for c in range(4):
+        cpk[c, 8:16, :] = zero8
+    for x in (0, 1, 22, 23):
+        for k in range(4):
+            fe[k, x, 8:16, :] = jnp.ones((8, 128), F32)
+            fe[k, x, 24:32, :] = jnp.ones((8, 128), F32)
     for copy in loads:
         copy.wait()
 
@@ -118,6 +145,13 @@
         return carry
 
     lax.fori_loop(0, 16, stage, 0)
+    for c, (dx, dy) in enumerate(CORNERS):
+        a, b = (13, 12) if dx > 0 else (2, 3)
+        y, edge = (14, 15) if dy > 0 else (0, 0)
+        for k in range(4):
+            cpk[c, 2 * k:2 * k + 2, :] = own[a * 4 + k, y:y + 2, :]
+        cpk[c, 8:9, :] = own[b * 4 + FX, edge:edge + 1, :]
+        cpk[c, 9:10, :] = own[b * 4 + CODE, edge:edge + 1, :]
     sides_x = 2 - (gx == 0).astype(jnp.int32) - x_last.astype(jnp.int32)
     sides_y = 2 - (gy == 0).astype(jnp.int32) - y_last.astype(jnp.int32)
     pl.semaphore_wait(barrier, 2 + len(far) + sides_x * (1 + sides_y))
@@ -159,18 +193,27 @@
         link(own.at[pl.ds(15, 1)], rxh.at[pl.ds(12, 1)], x_send.at[4], x_recv.at[4], -1, 0),
     ]
     near_corners, deep_corners = [], []
-    for corners, from_low, to_low, from_high, to_high in (
-            (near_corners, 224, 32, 0, 320), (deep_corners, 192, 0, 32, 352)):
-        for src, dst, dy in ((yph, ryl, 1), (ypl, ryh, -1)):
-            for dx, a, b in ((1, from_low, to_low), (-1, from_high, to_high)):
-                at = 2 + len(near_corners) + len(deep_corners)
-                corners.append(link(src.at[pl.ds(a, 32)], dst.at[pl.ds(b, 32)], y_send.at[at], y_recv.at[at], dx, dy))
+    for c, (dx, dy) in enumerate(CORNERS):
+        src, dst = (yph, ryl) if dy > 0 else (ypl, ryh)
+        a, b = (224, 32) if dx > 0 else (0, 320)
+        near_corners.append(
+            link(src.at[pl.ds(a, 32)], dst.at[pl.ds(b, 32)], y_send.at[2 + c], y_recv.at[2 + c], dx, dy))
+        deep_corners.append(link(cpk.at[c], crx.at[c], y_send.at[6 + c], y_recv.at[6 + c], dx, dy))
     start(near_copies)
     start(pad_copies)
     start(y_copies)
     start(near_corners)
     start(deep_copies)
     start(deep_corners)
+
+    for (dx, dy), c in zip(CORNERS, range(4)):
+        def fill(c=c, dy=dy):
+            crx[c] = jnp.ones((16, 128), F32)
+            if dy > 0:
+                crx[c, 2 * FY + 1:2 * FY + 2, :] = jnp.zeros((1, 128), F32)
+
+        pl.when(jnp.logical_not(inside(-dx, -dy)))(fill)
+
     near_copies += near_corners
     deep_copies += deep_corners
 
@@ -450,8 +493,13 @@
     for i in range(4):
         fe[i, 22, 12:28, :] = rxh[8 + i]
     fe[CODE, 23, 12:28, :] = rxh[12]
-    for x in (0, 1, 22, 23):
-        unpack(x)
+    for c, (dx, dy) in enumerate(CORNERS):
+        a, b = (1, 0) if dx > 0 else (22, 23)
+        y, edge = (10, 11) if dy > 0 else (28, 28)
+        for k in range(4):
+            fe[k, a, y:y + 2, :] = crx[c, 2 * k:2 * k + 2, :]
+        fe[FX, b, edge:edge + 1, :] = crx[c, 8:9, :]
+        fe[CODE, b, edge:edge + 1, :] = crx[c, 9:10, :]
     both(first, 0, 22, 2, 2)
     both(coefficients, 1, 22, 1, 1)
     coefficients(2)
@@ -470,7 +518,7 @@
     halves = []
     for up in range(2):
         gather = ((lane_tile == col + up) & (col < 16)).astype(F32)
-        z = dot(xs[...], gather)
+        z = dot_left(xs[...], gather)
         v = jnp.where(even, z[0:128] - z[128:256], z[128:256])
         other = jnp.where(even_row, pltpu.roll(v, 127, 0), pltpu.roll(v, 1, 0))
         halves.append(jnp.where(even, v, other))
@@ -533,6 +581,8 @@
                 pltpu.VMEM((256, 128), F32),
                 pltpu.VMEM((384, 128), F32),
                 pltpu.VMEM((384, 128), F32),
+                pltpu.VMEM((4, 16, 128), F32),
+                pltpu.VMEM((4, 16, 128), F32),
                 pltpu.VMEM((8, 128), F32),
                 pltpu.VMEM((64, 128), F32),
                 pltpu.VMEM((16, 128), F32),

time: 29.6 us -> 28.6 us (0.966)
  Pallas kernels: 28.9 us -> 27.8 us
    pallas_call x1, Pallas kernels: 27.9 us -> 26.8 us  [on_device(): pl.pallas_call(functools.partial(kernel, n_x, n_y), out_shape=(pltpu.VMEM...]
where the time goes in v5:
time: 28.6 us; the launch traced here: 28.5 us
  Pallas kernels  27.8 us (97%)
  between operations  0.64 us (2%)
    pallas_call x1, Pallas kernels, on_device(): pl.pallas_call(functools.partial(kernel, n_x, n_y), out_shape=(pltpu.VMEM...  26.8 us
    pallas_call x1, Pallas kernels, on_device(): pl.pallas_call(writer, out_shape=(jax.ShapeDtypeStruct((8, 16, 16, 128),...  0.99 us

profile of v5, /device:TPU:95, one launch (start us, length us, event | category | flops | bytes accessed | tf_op | source)
XLA Modules:
  0.0 28.5 jit_solution(12149974794276347711)
XLA Ops:
  0.6 26.8 %shard_map.59 = (f32[8,16,16,128]{3,2,1,0:T(8,128)S(1)}, f32[27,1,128]{2,1,0:T(1,128)S(1)}) custom-call(f32[3,16,16,128]{3,2,1,0:T(8,128)} %ft_in.1, s32[16,16,128]{2,1,0:T(8,128)} %pt_in.1, s32[6,2,2,16]{3,2,1,0:T(2,128)} %sp_in.1, s32[1,64]{1,0:T(1,128)} %bitcast.4), custom_call_target="tpu_custom_call" | custom-call | tf_op jit(solution)/shard_map/pallas_call | solution.py:564
  27.5 1.0 %shard_map.60 = (f32[8,16,16,128]{3,2,1,0:T(8,128)}, f32[27,1,128]{2,1,0:T(1,128)}) custom-call(f32[8,16,16,128]{3,2,1,0:T(8,128)S(1)} %get-tuple-element.6.pro, f32[27,1,128]{2,1,0:T(1,128)S(1)} %get-tuple-element.7.rows), custom_call_target="tpu_custom_call" | custom-call | tf_op jit(solution)/shard_map/pallas_call | solution.py:612

commit v6 on v5

--- a/solution.py
+++ b/solution.py
@@ -470,6 +470,8 @@
     weigh(2)
     layers(functools.partial(sums, 1), 0, 8, 4)
     layers(functools.partial(sums, 2), 0, 8, 4)
+    over_rows(1)
+    over_rows(2)
 
     arrive(near_copies)
     for i in range(8):
@@ -508,8 +510,8 @@
     both(apply, 3, 19, 2, 2)
     layers(functools.partial(sums, 0), 0, 8, 4)
     layers(functools.partial(sums, 3), 0, 8, 4)
-    for a in range(4):
-        over_rows(a)
+    over_rows(0)
+    over_rows(3)
 
     lane_tile = (iota((128, 128), 0) + 4) >> 3
     col = iota((128, 128), 1)
@@ -531,7 +533,7 @@
 
     mine = pl.multiple_of(gy * 8, 8)
     sent = []
-    for j in range(1, n_y):
+    for j in sorted(range(1, n_y), key=lambda j: abs(2 * j - n_y)):
         there = lax.rem(gy + j, n_y)
         copy = remote(snd.at[pl.ds(pl.multiple_of(there * 8, 8), 8)], rcv.at[pl.ds(mine, 8)],
                       e_send.at[j], e_recv.at[j], 0, j)

time: 28.6 us -> 28.5 us (level)
  no operation moved by 1% of the time
where the time goes in v6:
time: 28.5 us; the launch traced here: 28.4 us
  Pallas kernels  27.8 us (98%)
  between operations  0.64 us (2%)
    pallas_call x1, Pallas kernels, on_device(): pl.pallas_call(functools.partial(kernel, n_x, n_y), out_shape=(pltpu.VMEM...  26.8 us
    pallas_call x1, Pallas kernels, on_device(): pl.pallas_call(writer, out_shape=(jax.ShapeDtypeStruct((8, 16, 16, 128),...  0.99 us

profile of v6, /device:TPU:95, one launch (start us, length us, event | category | flops | bytes accessed | tf_op | source)
XLA Modules:
  0.0 28.4 jit_solution(306123831836086684)
XLA Ops:
  0.6 26.8 %shard_map.59 = (f32[8,16,16,128]{3,2,1,0:T(8,128)S(1)}, f32[27,1,128]{2,1,0:T(1,128)S(1)}) custom-call(f32[3,16,16,128]{3,2,1,0:T(8,128)} %ft_in.1, s32[16,16,128]{2,1,0:T(8,128)} %pt_in.1, s32[6,2,2,16]{3,2,1,0:T(2,128)} %sp_in.1, s32[1,64]{1,0:T(1,128)} %bitcast.4), custom_call_target="tpu_custom_call" | custom-call | tf_op jit(solution)/shard_map/pallas_call | solution.py:566
  27.4 1.0 %shard_map.60 = (f32[8,16,16,128]{3,2,1,0:T(8,128)}, f32[27,1,128]{2,1,0:T(1,128)}) custom-call(f32[8,16,16,128]{3,2,1,0:T(8,128)S(1)} %get-tuple-element.6.pro, f32[27,1,128]{2,1,0:T(1,128)S(1)} %get-tuple-element.7.rows), custom_call_target="tpu_custom_call" | custom-call | tf_op jit(solution)/shard_map/pallas_call | solution.py:614

commit v7 on v6

--- a/solution.py
+++ b/solution.py
@@ -201,8 +201,8 @@
         deep_corners.append(link(cpk.at[c], crx.at[c], y_send.at[6 + c], y_recv.at[6 + c], dx, dy))
     start(near_copies)
     start(pad_copies)
+    start(near_corners)
     start(y_copies)
-    start(near_corners)
     start(deep_copies)
     start(deep_corners)
 

time: 28.5 us -> 29 us (1.018)
  Pallas kernels: 27.8 us -> 28.3 us
    pallas_call x1, Pallas kernels: 26.8 us -> 27.3 us  [on_device(): pl.pallas_call(functools.partial(kernel, n_x, n_y), out_shape=(pltpu.VMEM...]
where the time goes in v7:
time: 29 us; the launch traced here: 28.9 us
  Pallas kernels  28.3 us (98%)
  between operations  0.64 us (2%)
    pallas_call x1, Pallas kernels, on_device(): pl.pallas_call(functools.partial(kernel, n_x, n_y), out_shape=(pltpu.VMEM...  27.3 us
    pallas_call x1, Pallas kernels, on_device(): pl.pallas_call(writer, out_shape=(jax.ShapeDtypeStruct((8, 16, 16, 128),...  0.99 us

profile of v7, /device:TPU:95, one launch (start us, length us, event | category | flops | bytes accessed | tf_op | source)
XLA Modules:
  0.0 28.9 jit_solution(6158611147344554543)
XLA Ops:
  0.6 27.3 %shard_map.59 = (f32[8,16,16,128]{3,2,1,0:T(8,128)S(1)}, f32[27,1,128]{2,1,0:T(1,128)S(1)}) custom-call(f32[3,16,16,128]{3,2,1,0:T(8,128)} %ft_in.1, s32[16,16,128]{2,1,0:T(8,128)} %pt_in.1, s32[6,2,2,16]{3,2,1,0:T(2,128)} %sp_in.1, s32[1,64]{1,0:T(1,128)} %bitcast.4), custom_call_target="tpu_custom_call" | custom-call | tf_op jit(solution)/shard_map/pallas_call | solution.py:566
  27.9 1.0 %shard_map.60 = (f32[8,16,16,128]{3,2,1,0:T(8,128)}, f32[27,1,128]{2,1,0:T(1,128)}) custom-call(f32[8,16,16,128]{3,2,1,0:T(8,128)S(1)} %get-tuple-element.6.pro, f32[27,1,128]{2,1,0:T(1,128)S(1)} %get-tuple-element.7.rows), custom_call_target="tpu_custom_call" | custom-call | tf_op jit(solution)/shard_map/pallas_call | solution.py:614
